TPU v7x, 128 devices: a whole 4x4x4 slice. The times are simulated.
128 devices in a mesh: wide: 16 (over z_hi, y, core), narrow: 8 (over z_lo, x).
Axes of the slice: x: 4, y: 4, z: 4 (z_hi: 2, z_lo: 2; z = z_hi * 2 + z_lo), core: 2. Of those that a mesh axis runs over, the one named last changes fastest.
Arguments:
- field: bfloat16 [32, 128, 128, 128], P(None, 'wide', 'narrow'), may hold values from -6 to 6
- spectral_weight: bfloat16 [48, 48, 48, 2048], P('wide', 'narrow'), may hold values from -3 to 3
- pointwise_weight: bfloat16 [32, 32], replicated, may hold values from -1 to 1
- cotangent: bfloat16 [32, 128, 128, 128], P(None, 'wide', 'narrow'), may hold values from -6 to 6
Outputs:
- activation: bfloat16 [32, 128, 128, 128], P(None, 'wide', 'narrow')
- field_grad: bfloat16 [32, 128, 128, 128], P(None, 'wide', 'narrow')
- weight_grad: bfloat16 [48, 48, 48, 2048], P('wide', 'narrow')
All inputs are finite; a program needn't handle non-finite values.
Results may differ from a plain program's by a relative error of at most 0.025.
Values may be sent and summed in bfloat16 or wider, within the bound.
A program may use at most 128 MiB of HBM per device.

v0:
```python
import functools

import jax
import jax.numpy as jnp
import ml_dtypes
import numpy as np
from jax import lax
from jax.experimental import pallas as pl
from jax.experimental.pallas import tpu as pltpu
from jax.sharding import PartitionSpec as P

C = 32
XL = 8
YL = 16
KXL = 6
KL = 3
NZ = 128
MESH = pl.DeviceIdType.MESH
F32 = jnp.float32
BF16 = jnp.bfloat16


def angles(extent, kept, two_sided):
    positions = np.arange(kept)
    frequency = (
        np.where(positions < kept // 2, positions, positions + extent - kept)
        if two_sided
        else positions
    )
    phases = np.arange(extent)[:, None] * frequency[None, :] % extent
    theta = 2.0 * np.pi * phases / extent
    rounded = lambda t: t.astype(np.float32).astype(ml_dtypes.bfloat16).astype(np.float32)
    return rounded(np.cos(theta)), rounded(np.sin(theta))


def tables(wide, narrow, ky):
    nx, ny, kx, kz = XL * wide, YL * narrow, KXL * narrow, KL * wide
    cx, sx = angles(nx, kx, True)
    cy, sy = angles(ny, ky, True)
    cz, sz = angles(NZ, kz, False)
    z_rows = np.stack([cz, -sz], axis=-1).reshape(NZ, wide, KL, 2)
    z_fwd = z_rows.transpose(2, 1, 3, 0).reshape(KL * wide * 2, NZ)
    z_inv = z_fwd
    fwd = lambda c, s: np.stack([np.stack([c, s]), np.stack([-s, c])])
    inv = lambda c, s: np.stack([np.stack([c, -s]), np.stack([s, c])])
    fx = fwd(cx, sx).reshape(2, 2, wide, XL, narrow, KXL)
    x_fwd = fx.transpose(5, 4, 0, 2, 1, 3).reshape(KXL * narrow * 2, wide * 2 * XL)
    ix = inv(cx, sx).reshape(2, 2, wide, XL, narrow, KXL)
    x_inv = ix.transpose(2, 0, 3, 5, 4, 1).reshape(wide * 2 * XL, KXL * narrow * 2)
    fy = fwd(cy, sy).reshape(2, 2, narrow, YL, ky)
    y_fwd = fy.transpose(0, 4, 2, 1, 3).reshape(2 * ky, narrow * 2 * YL)
    iy = inv(cy, sy).reshape(2, 2, narrow, YL, ky)
    y_inv = iy.transpose(2, 0, 3, 1, 4).reshape(narrow * 2 * YL, 2 * ky)
    return [t.astype(ml_dtypes.bfloat16) for t in (z_fwd, z_inv, x_fwd, x_inv, y_fwd, y_inv)]


def dot(a, b, dims=((1,), (0,))):
    return lax.dot_general(a, b, (dims, ((), ())), preferred_element_type=F32)


def ones_where(condition):
    return jnp.where(condition, 1.0, 0.0).astype(BF16)


def kernel(
    wide, narrow, ky, total,
    field, cot_hbm, weight_hbm, pw, z_fwd, z_inv, x_fwd, x_inv, y_fwd, y_inv,
    act_hbm, fgrad_hbm, wgrad_hbm,
    cot, weight, act, fgrad, wgrad,
    zs, zi, near, slope, spec, mix, t1, t2,
    perm, perm_t, pw_fwd, pw_back, repeat, tile, group_sum,
    ws, wr, ns, nr,
    ws_sem, wr_sem, ns_sem, nr_sem, load_sem, store_sem,
):
    w = lax.axis_index("wide")
    n = lax.axis_index("narrow")
    cells = C * YL
    pairs = 2 * narrow
    kk = KL * wide * 2

    load_cot = pltpu.make_async_copy(cot_hbm, cot, load_sem.at[0])
    load_weight = pltpu.make_async_copy(weight_hbm, weight, load_sem.at[1])
    load_cot.start()
    load_weight.start()

    barrier = pltpu.get_barrier_semaphore()

    @pl.loop(1, wide)
    def _(d):
        pl.semaphore_signal(
            barrier, inc=1, device_id={"wide": lax.rem(w + d, wide)}, device_id_type=MESH
        )

    @pl.loop(1, narrow)
    def _(d):
        pl.semaphore_signal(
            barrier, inc=1, device_id={"narrow": lax.rem(n + d, narrow)}, device_id_type=MESH
        )

    row = lax.broadcasted_iota(jnp.int32, (cells, cells), 0)
    col = lax.broadcasted_iota(jnp.int32, (cells, cells), 1)
    perm[...] = ones_where(((row & 15) == (col >> 5)) & ((row >> 4) == (col & 31)))

    lane = lax.broadcasted_iota(jnp.int32, (1, 128), 1) >> 5

    def depth(x, b, block):
        out = dot(z_fwd[...], block, ((1,), (1,)))
        zs[b, pl.ds(x, kk, stride=XL), :] = out

    def send_wide(a, j):
        wr[a, j, w] = ws[a, j, w]

        @pl.loop(1, wide)
        def _(d):
            to = lax.rem(w + d, wide)
            pltpu.make_async_remote_copy(
                src_ref=ws.at[a, j, to],
                dst_ref=wr.at[a, j, w],
                send_sem=ws_sem.at[a, j],
                recv_sem=wr_sem.at[a, j],
                device_id={"wide": to},
                device_id_type=MESH,
            ).start()

    def send_narrow(a, j):
        nr[a, j, n] = ns[a, j, n]

        @pl.loop(1, narrow)
        def _(d):
            to = lax.rem(n + d, narrow)
            pltpu.make_async_remote_copy(
                src_ref=ns.at[a, j, to],
                dst_ref=nr.at[a, j, n],
                send_sem=ns_sem.at[a, j],
                recv_sem=nr_sem.at[a, j],
                device_id={"narrow": to},
                device_id_type=MESH,
            ).start()

    def wait_all(buffer, a, j, sem, count):
        ref = buffer.at[a, j, pl.ds(0, count - 1)]
        pltpu.make_async_copy(ref, ref, sem.at[a, j]).wait()

    def depth_out(a, j):
        rows = pl.ds(j * wide * 16, wide * 16)
        block = jnp.concatenate([zs[b, rows, :].astype(BF16) for b in range(4)], axis=1)
        out = dot(block, perm[...]).astype(BF16)
        ws[a, j] = out.reshape(wide, 16, cells)
        send_wide(a, j)

    def x_forward(a, j):
        wait_all(wr, a, j, wr_sem, wide)
        out = dot(x_fwd[...], wr[a, j].reshape(wide * 16, cells))
        for y in range(YL):
            yb, g = y // 4, y % 4
            for lb in range(2):
                acc = None
                for s in range(4 if lb == 0 else 2):
                    kx = 4 * lb + s
                    piece = out[kx * pairs : (kx + 1) * pairs, yb * 128 : (yb + 1) * 128]
                    if s != g:
                        piece = pltpu.roll(piece, ((s - g) * 32) % 128, 1)
                    acc = piece if acc is None else jnp.where(lane == s, piece, acc)
                t1[lb, pl.ds(y, pairs, stride=YL), :] = acc
        for lb in range(2):
            ns[a, j, :, :, lb * 128 : (lb + 1) * 128] = (
                t1[lb].astype(BF16).reshape(narrow, 2 * YL, 128)
            )
        send_narrow(a, j)

    def y_forward(a, j, which):
        wait_all(nr, a, j, nr_sem, narrow)
        out = dot(y_fwd[...], nr[a, j].reshape(narrow * 2 * YL, 256)).astype(BF16)
        for lb in range(2):
            spec[which, j, lb] = out[:, lb * 128 : (lb + 1) * 128]

    def scale(j):
        return jnp.where(w * KL + j == 0, 1.0, 2.0).astype(F32) / total

    def channels_first(which, j, kx):
        rolled = pltpu.roll(
            spec[which, j, kx // 4].astype(F32), lax.rem(128 - 32 * lax.rem(kx, 4), 128), 1
        )
        return rolled.astype(BF16)

    def place(kx, value):
        lb = kx // 4
        mix[lb] = jnp.where(lane == lax.rem(kx, 4), value, mix[lb])

    def mix_forward(j):
        @pl.loop(0, KXL)
        def _(kx):
            spectrum = channels_first(0, j, kx)
            acc_r = jnp.zeros((ky, 128), F32)
            acc_i = jnp.zeros((ky, 128), F32)
            for b in range(4):
                lanes = slice(b * 256, (b + 1) * 256)
                rep = dot(spectrum, repeat[:, lanes])
                rep_r, rep_i = rep[:ky], rep[ky:]
                w_r = weight[j, kx, :, b * 256 : (b + 1) * 256].astype(F32)
                w_i = weight[j, kx, :, 1024 + b * 256 : 1024 + (b + 1) * 256].astype(F32)
                p_r = rep_r * w_r - rep_i * w_i
                p_i = rep_r * w_i + rep_i * w_r
                acc_r = acc_r + (p_r[:, :128] + p_r[:, 128:])
                acc_i = acc_i + (p_i[:, :128] + p_i[:, 128:])
            acc = jnp.concatenate([acc_r, acc_i], axis=0) * scale(j)
            acc = acc + pltpu.roll(acc, 64, 1)
            acc = acc + pltpu.roll(acc, 32, 1)
            place(kx, acc)

    def mix_back(j):
        @pl.loop(0, KXL)
        def _(kx):
            tiled = dot(channels_first(1, j, kx), tile[...])
            g_r = jnp.concatenate([tiled[:ky]] * 2, axis=1)
            g_i = jnp.concatenate([tiled[ky:]] * 2, axis=1)
            acc = jnp.zeros((2 * ky, 128), F32)
            for b in range(4):
                w_r = weight[j, kx, :, b * 256 : (b + 1) * 256].astype(F32)
                w_i = weight[j, kx, :, 1024 + b * 256 : 1024 + (b + 1) * 256].astype(F32)
                a_r = (w_r * g_r + w_i * g_i).astype(BF16)
                a_i = (w_r * g_i - w_i * g_r).astype(BF16)
                acc = acc + dot(
                    jnp.concatenate([a_r, a_i], axis=0), group_sum[b * 256 : (b + 1) * 256, :]
                )
            place(kx, acc * scale(j))

    def weight_gradient(j):
        @pl.loop(0, KXL)
        def _(kx):
            spectrum = channels_first(0, j, kx)
            tiled = dot(channels_first(1, j, kx), tile[...]) * scale(j)
            g_r = jnp.concatenate([tiled[:ky]] * 2, axis=1)
            g_i = jnp.concatenate([tiled[ky:]] * 2, axis=1)
            for b in range(4):
                rep = dot(spectrum, repeat[:, b * 256 : (b + 1) * 256])
                rep_r, rep_i = rep[:ky], rep[ky:]
                wgrad[j, kx, :, b * 256 : (b + 1) * 256] = (rep_r * g_r + rep_i * g_i).astype(BF16)
                wgrad[j, kx, :, 1024 + b * 256 : 1024 + (b + 1) * 256] = (
                    rep_r * g_i - rep_i * g_r
                ).astype(BF16)

    def y_inverse(a, j):
        modes = jnp.concatenate([mix[0].astype(BF16), mix[1].astype(BF16)], axis=1)
        out = dot(y_inv[...], modes).astype(BF16)
        ns[a, j] = out.reshape(narrow, 2 * YL, 256)
        send_narrow(a, j)

    def x_inverse(a, j, aw):
        wait_all(nr, a, j, nr_sem, narrow)
        for lb in range(2):
            t1[lb] = (
                nr[a, j, :, :, lb * 128 : (lb + 1) * 128]
                .reshape(narrow * 2 * YL, 128)
                .astype(F32)
            )
        for yb in range(4):
            for lb in range(2):
                loaded = [t1[lb, pl.ds(4 * yb + g, pairs, stride=YL), :] for g in range(4)]
                for s in range(4 if lb == 0 else 2):
                    kx = 4 * lb + s
                    acc = None
                    for g in range(4):
                        piece = loaded[g]
                        if s != g:
                            piece = pltpu.roll(piece, ((g - s) * 32) % 128, 1)
                        acc = piece if acc is None else jnp.where(lane == g, piece, acc)
                    t2[kx * pairs : (kx + 1) * pairs, yb * 128 : (yb + 1) * 128] = acc.astype(BF16)
        out = dot(x_inv[...], t2[...]).astype(BF16)
        ws[aw, j] = out.reshape(wide, 16, cells)
        send_wide(aw, j)

    def depth_in(a, j):
        wait_all(wr, a, j, wr_sem, wide)
        out = dot(wr[a, j].reshape(wide * 16, cells), perm_t[...])
        for b in range(4):
            zi[b, pl.ds(j * wide * 16, wide * 16), :] = out[:, b * 128 : (b + 1) * 128]

    def depth_inverse(x, b):
        block = zi[b, pl.ds(x, kk, stride=XL), :].astype(BF16)
        return dot(block, z_inv[...], ((0,), (0,)))

    def pointwise(matrix, source):
        @pl.loop(0, XL)
        def _(x):
            near[x] = dot(matrix[...], source[:, x].reshape(cells, NZ))

    for x in range(XL):
        plane = field[:, x].reshape(cells, NZ)
        for b in range(4):
            depth(x, b, plane[b * 128 : (b + 1) * 128])

    pl.semaphore_wait(barrier, wide + narrow - 2)

    for j in range(KL):
        depth_out(0, j)

    perm_t[...] = ones_where(((row >> 5) == (col & 15)) & ((row & 31) == (col >> 4)))
    spread_row = lax.broadcasted_iota(jnp.int32, (cells, C), 0)
    spread_col = lax.broadcasted_iota(jnp.int32, (cells, C), 1)
    spread = ones_where((spread_row >> 4) == spread_col)
    same_y = (row & 15) == (col & 15)
    back = dot(dot(spread, pw[...]).astype(BF16), spread, ((1,), (1,)))
    pw_back[...] = jnp.where(same_y, back, 0.0).astype(BF16)
    ahead = dot(dot(spread, pw[...], ((1,), (1,))).astype(BF16), spread, ((1,), (1,)))
    pw_fwd[...] = jnp.where(same_y, ahead, 0.0).astype(BF16)
    r_row = lax.broadcasted_iota(jnp.int32, (128, 1024), 0)
    r_col = lax.broadcasted_iota(jnp.int32, (128, 1024), 1)
    repeat[...] = ones_where(r_row == (r_col >> 5))
    t_row = lax.broadcasted_iota(jnp.int32, (128, 128), 0)
    t_col = lax.broadcasted_iota(jnp.int32, (128, 128), 1)
    tile[...] = ones_where(t_row == (t_col & 31))
    g_row = lax.broadcasted_iota(jnp.int32, (1024, 128), 0)
    g_col = lax.broadcasted_iota(jnp.int32, (1024, 128), 1)
    group_sum[...] = ones_where((g_row >> 5) == (g_col & 31))
    mix[...] = jnp.zeros_like(mix)
    pointwise(pw_fwd, field)
    load_weight.wait()

    for j in range(KL):
        x_forward(0, j)
    for j in range(KL):
        y_forward(0, j, 0)
        mix_forward(j)
        y_inverse(1, j)
    for j in range(KL):
        x_inverse(1, j, 1)
    load_cot.wait()
    for j in range(KL):
        depth_in(1, j)

    root = 0.7978845608028654

    @pl.loop(0, 4)
    def _(b):
        rows = pl.ds(pl.multiple_of(b * 128, 128), 128)
        group = pl.ds(b * 8, 8)
        for x in range(XL):
            t = depth_inverse(x, b) + near[x, rows, :]
            square = t * t
            th = jnp.tanh(root * t * (1.0 + 0.044715 * square))
            half = 0.5 + 0.5 * th
            act[group, x] = (t * half).astype(BF16).reshape(8, YL, NZ)
            grad = half + (0.5 * root) * t * (1.0 - th * th) * (1.0 + 0.134145 * square)
            up = cot[group, x].reshape(128, NZ).astype(F32)
            block = (up * grad).astype(BF16)
            slope[group, x] = block.reshape(8, YL, NZ)
            depth(x, b, block)

    store_act = pltpu.make_async_copy(act, act_hbm, store_sem.at[0])
    store_act.start()

    for j in range(KL):
        depth_out(2, j)
    pointwise(pw_back, slope)
    for j in range(KL):
        x_forward(2, j)
    for j in range(KL):
        y_forward(2, j, 1)
        mix_back(j)
        y_inverse(3, j)
    for j in range(KL):
        x_inverse(3, j, 3)
    for j in range(KL):
        weight_gradient(j)
    store_wgrad = pltpu.make_async_copy(wgrad, wgrad_hbm, store_sem.at[1])
    store_wgrad.start()
    for j in range(KL):
        depth_in(3, j)

    @pl.loop(0, 4)
    def _(b):
        rows = pl.ds(pl.multiple_of(b * 128, 128), 128)
        group = pl.ds(b * 8, 8)
        for x in range(XL):
            t = depth_inverse(x, b) + near[x, rows, :]
            fgrad[group, x] = t.astype(BF16).reshape(8, YL, NZ)

    store_fgrad = pltpu.make_async_copy(fgrad, fgrad_hbm, store_sem.at[2])
    store_fgrad.start()

    for a in range(4):
        for j in range(KL):
            wait_all(ws, a, j, ws_sem, wide)
            wait_all(ns, a, j, ns_sem, narrow)
    store_act.wait()
    store_wgrad.wait()
    store_fgrad.wait()


def on_device(wide, narrow, field, weight, pw, cot):
    ky = weight.shape[2]
    total = float(XL * wide * YL * narrow * NZ)
    consts = tables(wide, narrow, ky)
    cells = C * YL
    kk = KL * wide * 2
    vmem = pl.BlockSpec(memory_space=pltpu.VMEM)
    hbm = pl.BlockSpec(memory_space=pl.ANY)
    act, fgrad, wgrad = pl.pallas_call(
        functools.partial(kernel, wide, narrow, ky, total),
        out_shape=(
            jax.ShapeDtypeStruct(field.shape, BF16),
            jax.ShapeDtypeStruct(field.shape, BF16),
            jax.ShapeDtypeStruct(weight.shape, BF16),
        ),
        in_specs=[vmem, hbm, hbm, vmem] + [vmem] * 6,
        out_specs=(hbm, hbm, hbm),
        scratch_shapes=[
            pltpu.VMEM(cot.shape, BF16),
            pltpu.VMEM(weight.shape, BF16),
            pltpu.VMEM(field.shape, BF16),
            pltpu.VMEM(field.shape, BF16),
            pltpu.VMEM(weight.shape, BF16),
            pltpu.VMEM((4, kk * XL, 128), F32),
            pltpu.VMEM((4, kk * XL, 128), F32),
            pltpu.VMEM((XL, cells, NZ), F32),
            pltpu.VMEM(field.shape, BF16),
            pltpu.VMEM((2, KL, 2, 2 * ky, 128), BF16),
            pltpu.VMEM((2, 2 * ky, 128), F32),
            pltpu.VMEM((2, narrow * 2 * YL, 128), F32),
            pltpu.VMEM((KXL * narrow * 2, cells), BF16),
            pltpu.VMEM((cells, cells), BF16),
            pltpu.VMEM((cells, cells), BF16),
            pltpu.VMEM((cells, cells), BF16),
            pltpu.VMEM((cells, cells), BF16),
            pltpu.VMEM((128, 1024), BF16),
            pltpu.VMEM((128, 128), BF16),
            pltpu.VMEM((1024, 128), BF16),
            pltpu.VMEM((4, KL, wide, 2 * XL, cells), BF16),
            pltpu.VMEM((4, KL, wide, 2 * XL, cells), BF16),
            pltpu.VMEM((4, KL, narrow, 2 * YL, 256), BF16),
            pltpu.VMEM((4, KL, narrow, 2 * YL, 256), BF16),
            pltpu.SemaphoreType.DMA((4, KL)),
            pltpu.SemaphoreType.DMA((4, KL)),
            pltpu.SemaphoreType.DMA((4, KL)),
            pltpu.SemaphoreType.DMA((4, KL)),
            pltpu.SemaphoreType.DMA((2,)),
            pltpu.SemaphoreType.DMA((3,)),
        ],
        compiler_params=pltpu.CompilerParams(
            collective_id=0, has_side_effects=True, vmem_limit_bytes=48 * 1024 * 1024
        ),
        name="spectral_layer",
    )(field, cot, weight, pw, *[jnp.asarray(t) for t in consts])
    return act, fgrad, wgrad


def solution(mesh):
    wide, narrow = mesh.shape["wide"], mesh.shape["narrow"]
    return jax.shard_map(
        functools.partial(on_device, wide, narrow),
        mesh=mesh,
        in_specs=(
            P(None, "wide", "narrow", None),
            P("wide", "narrow", None, None),
            P(),
            P(None, "wide", "narrow", None),
        ),
        out_specs=(
            P(None, "wide", "narrow", None),
            P(None, "wide", "narrow", None),
            P("wide", "narrow", None, None),
        ),
        check_vma=False,
    )
```

profile of v0, /device:TPU:1, one launch (start us, length us, event | category | flops | bytes accessed | tf_op | source)
XLA Modules:
  0.0 99.2 jit_solution(10875547156641281943)
XLA Ops:
  0.6 0.0 copy-start
  0.6 1.2 %copy-done = bf16[32,8,16,128]{3,2,1,0:T(8,128)(2,1)S(1)} copy-done((bf16[32,8,16,128]{3,2,1,0:T(8,128)(2,1)S(1)}, bf16[32,8,16,128]{3,2,1,0:T(8,128)(2,1)}, u32[]{:S(2)}) %copy-start) | copy-done | bytes 1048600
  1.9 0.0 copy-start.1
  1.9 1.2 %copy-done.1 = bf16[32,8,16,128]{3,2,1,0:T(8,128)(2,1)S(1)} copy-done((bf16[32,8,16,128]{3,2,1,0:T(8,128)(2,1)S(1)}, bf16[32,8,16,128]{3,2,1,0:T(8,128)(2,1)}, u32[]{:S(2)}) %copy-start.1) | copy-done | bytes 1048600
  3.1 0.0 copy-start.2
  3.1 0.7 copy-done.2
  3.8 0.0 copy-start.3
  3.8 0.8 copy-done.3
  4.7 0.0 copy-start.4
  4.7 0.8 copy-done.4
  5.5 0.0 copy-start.5
  5.5 0.8 copy-done.5
  6.3 0.0 copy-start.6
  6.3 0.8 copy-done.6
  7.1 0.0 copy-start.7
  7.1 0.7 copy-done.7
  7.8 86.9 %spectral_layer.1 = (bf16[32,8,16,128]{3,2,1,0:T(8,128)(2,1)S(1)}, bf16[32,8,16,128]{3,2,1,0:T(8,128)(2,1)S(1)}, bf16[3,6,48,2048]{3,2,1,0:T(8,128)(2,1)}) custom-call(bf16[32,8,16,128]{3,2,1,0:T(8,128)(2,1)S(1)} %copy-done, bf16[32,8,16,128]{3,2,1,0:T(8,128)(2,1)S(1)} %copy-done.1, bf16[3,6,48,2048]{3,2,1,0:T(8,128)(2,1)} %weight_hbm.1, ...), custom_call_target="tpu_custom_call" | custom-call | tf_op jit(solution)/shard_map/spectral_layer/pallas_call | solution.py:399
  94.7 0.0 copy-start.8
  94.7 1.0 copy.16
  95.6 1.0 copy.17
  96.6 0.8 copy-done.8
  97.4 1.8 %copy.18 = bf16[3,6,48,2048]{3,2,1,0:T(8,128)(2,1)} copy(bf16[3,6,48,2048]{3,2,1,0:T(8,128)(2,1)S(1)} %copy-done.8) | data formatting | bytes 7077888
Async XLA Ops:
  0.6 1.2 %copy-start = (bf16[32,8,16,128]{3,2,1,0:T(8,128)(2,1)S(1)}, bf16[32,8,16,128]{3,2,1,0:T(8,128)(2,1)}, u32[]{:S(2)}) copy-start(bf16[32,8,16,128]{3,2,1,0:T(8,128)(2,1)} %field.1) | copy-start | bytes 3145732
  1.9 1.2 %copy-start.1 = (bf16[32,8,16,128]{3,2,1,0:T(8,128)(2,1)S(1)}, bf16[32,8,16,128]{3,2,1,0:T(8,128)(2,1)}, u32[]{:S(2)}) copy-start(bf16[32,8,16,128]{3,2,1,0:T(8,128)(2,1)} %cot_hbm.1) | copy-start | bytes 3145732
  3.1 0.7 copy-start.2
  3.8 0.8 copy-start.3
  4.7 0.8 copy-start.4
  5.5 0.8 copy-start.5
  6.3 0.8 copy-start.6
  7.1 0.7 copy-start.7
  94.7 2.8 %copy-start.8 = (bf16[3,6,48,2048]{3,2,1,0:T(8,128)(2,1)S(1)}, bf16[3,6,48,2048]{3,2,1,0:T(8,128)(2,1)}, u32[]{:S(2)}) copy-start(bf16[3,6,48,2048]{3,2,1,0:T(8,128)(2,1)} %get-tuple-element.8) | copy-start | bytes 10616836
where the time goes:
time: 99.7 us; the launch traced here: 99.2 us
  Pallas kernels  86.9 us (87%)
  local copies, waits for them, and re-layouts  11.7 us (12%)
    pallas_call x1, Pallas kernels, on_device(): pl.pallas_call(functools.partial(kernel, wide, narrow, ky, total), out_sh...  86.9 us
    unnamed x21, local copies, waits for them, and re-layouts  11.7 us

commit v1 on v0

v1 whole, which is shorter than its diff:
```python
import functools

import jax
import jax.numpy as jnp
import ml_dtypes
import numpy as np
from jax import lax
from jax.experimental import pallas as pl
from jax.experimental.pallas import tpu as pltpu
from jax.sharding import PartitionSpec as P

C = 32
XL = 8
YL = 16
KXL = 6
KL = 3
NZ = 128
VMEM_BYTES = 64 * 1024 * 1024
MESH = pl.DeviceIdType.MESH
F32 = jnp.float32
BF16 = jnp.bfloat16


def angles(extent, kept, two_sided):
    positions = np.arange(kept)
    frequency = (
        np.where(positions < kept // 2, positions, positions + extent - kept)
        if two_sided
        else positions
    )
    phases = np.arange(extent)[:, None] * frequency[None, :] % extent
    theta = 2.0 * np.pi * phases / extent
    rounded = lambda t: t.astype(np.float32).astype(ml_dtypes.bfloat16).astype(np.float32)
    return rounded(np.cos(theta)), rounded(np.sin(theta))


def tables(wide, narrow, ky):
    nx, ny, kx, kz = XL * wide, YL * narrow, KXL * narrow, KL * wide
    cx, sx = angles(nx, kx, True)
    cy, sy = angles(ny, ky, True)
    cz, sz = angles(NZ, kz, False)
    z_rows = np.stack([cz, -sz], axis=-1).reshape(NZ, wide, KL, 2)
    z_fwd = z_rows.transpose(2, 1, 3, 0).reshape(KL * wide * 2, NZ)
    fwd = lambda c, s: np.stack([np.stack([c, s]), np.stack([-s, c])])
    inv = lambda c, s: np.stack([np.stack([c, -s]), np.stack([s, c])])
    fx = fwd(cx, sx).reshape(2, 2, wide, XL, narrow, KXL)
    x_fwd = fx.transpose(5, 0, 4, 2, 1, 3).reshape(KXL * 2 * narrow, wide * 2 * XL)
    ix = inv(cx, sx).reshape(2, 2, wide, XL, narrow, KXL)
    x_inv = ix.transpose(2, 0, 3, 5, 1, 4).reshape(wide * 2 * XL, KXL * 2 * narrow)
    fy = fwd(cy, sy).reshape(2, 2, narrow, YL, ky)
    y_fwd = fy.transpose(0, 4, 2, 1, 3).reshape(2 * ky, narrow * 2 * YL)
    y_fwd_split = fy.transpose(1, 0, 4, 2, 3).reshape(4 * ky, narrow * YL)
    iy = inv(cy, sy).reshape(2, 2, narrow, YL, ky)
    y_inv = iy.transpose(2, 0, 3, 1, 4).reshape(narrow * 2 * YL, 2 * ky)
    y_inv_split = iy.transpose(0, 2, 3, 1, 4).reshape(2 * narrow * YL, 2 * ky)
    found = (z_fwd, x_fwd, x_inv, y_fwd, y_fwd_split, y_inv, y_inv_split)
    places, blocks, row = [], [], 0
    for t in found:
        rows, columns = t.shape
        places.append((row, rows, columns))
        for first in range(0, columns, 128):
            block = t[:, first : first + 128]
            blocks.append(np.pad(block, ((0, 0), (0, 128 - block.shape[1]))))
            row += rows
    return places, np.concatenate(blocks).astype(ml_dtypes.bfloat16)


def read_table(table, place):
    row, rows, columns = place
    blocks = [
        table[row + i * rows : row + (i + 1) * rows, : min(128, columns - first)]
        for i, first in enumerate(range(0, columns, 128))
    ]
    return jnp.concatenate(blocks, axis=1) if len(blocks) > 1 else blocks[0]


def dot(a, b, dims=((1,), (0,))):
    return lax.dot_general(a, b, (dims, ((), ())), preferred_element_type=F32)


def ones_where(condition):
    return jnp.where(condition, 1.0, 0.0).astype(BF16)


def kernel(
    wide, narrow, ky, total, places,
    field_hbm, cot_hbm, weight_hbm, pw_hbm, table_hbm,
    act_hbm, wgrad_hbm, back_hbm, near_hbm,
    *scratch,
):
    (
        table, field, cot, weight, pw, act, wgrad, zi, near, back_rows, zs, slope, spec, sums, prods, mix, t1, t1_last, t2,
        perm, perm_t, pw_fwd, pw_back, repeat, tile, group_sum,
        ws, wr, ns, nr,
        ws_sem, wr_sem, ns_sem, nr_sem, load_sem, store_sem,
    ) = scratch
    w = lax.axis_index("wide")
    n = lax.axis_index("narrow")
    cells = C * YL
    kk = KL * wide * 2
    rows_j = wide * 2 * XL
    modes = KXL * 2 * ky

    z_fwd, x_fwd, x_inv, y_fwd, y_fwd_split, y_inv, y_inv_split = [
        functools.partial(read_table, table, place) for place in places
    ]
    z_part = pl.ds(0, kk)
    other = pl.ds(kk, table.shape[0] - kk)
    loads = [
        pltpu.make_async_copy(src, dst, load_sem.at[i])
        for i, (src, dst) in enumerate(
            (
                (field_hbm, field),
                (table_hbm.at[z_part], table.at[z_part]),
                (pw_hbm, pw),
                (table_hbm.at[other], table.at[other]),
                (cot_hbm, cot),
                (weight_hbm, weight),
            )
        )
    ]
    for load in loads:
        load.start()

    barrier = pltpu.get_barrier_semaphore()

    @pl.loop(1, wide)
    def _(d):
        pl.semaphore_signal(
            barrier, inc=1, device_id={"wide": lax.rem(w + d, wide)}, device_id_type=MESH
        )

    @pl.loop(1, narrow)
    def _(d):
        pl.semaphore_signal(
            barrier, inc=1, device_id={"narrow": lax.rem(n + d, narrow)}, device_id_type=MESH
        )

    row = lax.broadcasted_iota(jnp.int32, (cells, cells), 0)
    col = lax.broadcasted_iota(jnp.int32, (cells, cells), 1)
    perm[...] = ones_where(((row & 15) == (col >> 5)) & ((row >> 4) == (col & 31)))

    lane = lax.broadcasted_iota(jnp.int32, (1, 128), 1) >> 5

    def shift(value, groups):
        amount = (groups * 32) % 128
        return value if amount == 0 else pltpu.roll(value, amount, 1)

    def pick(pieces):
        acc = pieces[0]
        for s, piece in enumerate(pieces[1:], 1):
            acc = jnp.where(lane == s, piece, acc)
        return acc

    def depth(x, b, block):
        out = dot(z_fwd(), block, ((1,), (1,)))
        zs[b, pl.ds(x, kk, stride=XL), :] = out

    def send(axis, count, me, src, dst, send_sem, recv_sem, a, j):
        dst[a, j, me] = src[a, j, me]

        @pl.loop(1, count)
        def _(d):
            to = lax.rem(me + d, count)
            pltpu.make_async_remote_copy(
                src_ref=src.at[a, j, to],
                dst_ref=dst.at[a, j, me],
                send_sem=send_sem.at[a, j],
                recv_sem=recv_sem.at[a, j],
                device_id={axis: to},
                device_id_type=MESH,
            ).start()

    def send_wide(a, j):
        send("wide", wide, w, ws, wr, ws_sem, wr_sem, a, j)

    def send_narrow(a, j):
        send("narrow", narrow, n, ns, nr, ns_sem, nr_sem, a, j)

    def wait_all(buffer, a, j, sem, count):
        ref = buffer.at[a, j, pl.ds(0, count - 1)]
        pltpu.make_async_copy(ref, ref, sem.at[a, j]).wait()

    def part(j):
        return pl.ds(pl.multiple_of(j * rows_j, rows_j), rows_j)

    def depth_out(a):
        @pl.loop(0, KL)
        def _(j):
            block = jnp.concatenate([zs[b, part(j), :].astype(BF16) for b in range(4)], axis=1)
            ws[a, j] = dot(block, perm[...]).astype(BF16).reshape(wide, 2 * XL, cells)
            send_wide(a, j)

    def x_forward(a, j):
        wait_all(wr, a, j, wr_sem, wide)
        out = dot(x_fwd(), wr[a, j].reshape(rows_j, cells))
        for y in range(YL):
            yb, g = y // 4, y % 4

            def piece(kx, ri):
                first = (kx * 2 + ri) * narrow
                return out[first : first + narrow, yb * 128 : (yb + 1) * 128]

            for ri in range(2):
                t1[pl.ds(ri * YL + y, narrow, stride=2 * YL), :] = pick(
                    [shift(piece(s, ri), s - g) for s in range(4)]
                )
            t1_last[pl.ds(y, narrow, stride=YL), :] = pick(
                [shift(piece(4 + s % 2, s // 2), s - g) for s in range(4)]
            )
        ns[a, j, :, : 2 * YL, :] = t1[...].astype(BF16).reshape(narrow, 2 * YL, 128)
        ns[a, j, :, 2 * YL :, :] = t1_last[...].astype(BF16).reshape(narrow, YL, 128)
        send_narrow(a, j)

    def y_forward(a, j, which):
        wait_all(nr, a, j, nr_sem, narrow)
        first = dot(y_fwd(), nr[a, j, :, : 2 * YL, :].reshape(narrow * 2 * YL, 128))
        both = dot(y_fwd_split(), nr[a, j, :, 2 * YL :, :].reshape(narrow * YL, 128))
        last = both[: 2 * ky] + shift(both[2 * ky :], 2)
        for kx in range(KXL):
            source = first if kx < 4 else last
            spec[which, j, kx * 2 * ky : (kx + 1) * 2 * ky, :] = shift(source, -(kx % 4)).astype(BF16)

    def scale(j):
        return jnp.where(w * KL + j == 0, 1.0, 2.0).astype(F32) / total

    def weights(j, kx, b):
        return (
            weight[j, kx, :, b * 256 : (b + 1) * 256].astype(F32),
            weight[j, kx, :, 1024 + b * 256 : 1024 + (b + 1) * 256].astype(F32),
        )

    def mode_rows(kx):
        return slice(kx * 2 * ky, kx * 2 * ky + ky), slice(kx * 2 * ky + ky, (kx + 1) * 2 * ky)

    def place(summed):
        for lb in range(2):
            found = [
                summed[kx * 2 * ky : (kx + 1) * 2 * ky] for kx in range(4 * lb, min(4 * lb + 4, KXL))
            ]
            mix[lb] = pick(found).astype(BF16)

    def mix_forward(j):
        for b in range(4):
            rep = dot(spec[0, j], repeat[:, b * 256 : (b + 1) * 256])
            for kx in range(KXL):
                re, im = mode_rows(kx)
                w_r, w_i = weights(j, kx, b)
                p_r = rep[re] * w_r - rep[im] * w_i
                p_i = rep[re] * w_i + rep[im] * w_r
                p_r = p_r[:, :128] + p_r[:, 128:]
                p_i = p_i[:, :128] + p_i[:, 128:]
                sums[re, :] = p_r if b == 0 else sums[re, :] + p_r
                sums[im, :] = p_i if b == 0 else sums[im, :] + p_i
        acc = sums[...] * scale(j)
        acc = acc + shift(acc, 2)
        acc = acc + shift(acc, 1)
        place(acc)

    def mix_back(j):
        sums[...] = dot(spec[1, j], tile[...])
        for kx in range(KXL):
            re, im = mode_rows(kx)
            g_r = jnp.concatenate([sums[re, :]] * 2, axis=1)
            g_i = jnp.concatenate([sums[im, :]] * 2, axis=1)
            for b in range(4):
                w_r, w_i = weights(j, kx, b)
                lanes = slice(b * 256, (b + 1) * 256)
                prods[re, lanes] = (w_r * g_r + w_i * g_i).astype(BF16)
                prods[im, lanes] = (w_r * g_i - w_i * g_r).astype(BF16)
        place(dot(prods[...], group_sum[...]) * scale(j))

    def weight_gradient(j):
        sums[...] = dot(spec[1, j], tile[...]) * scale(j)
        for b in range(4):
            rep = dot(spec[0, j], repeat[:, b * 256 : (b + 1) * 256])
            for kx in range(KXL):
                re, im = mode_rows(kx)
                g_r = jnp.concatenate([sums[re, :]] * 2, axis=1)
                g_i = jnp.concatenate([sums[im, :]] * 2, axis=1)
                wgrad[j, kx, :, b * 256 : (b + 1) * 256] = (rep[re] * g_r + rep[im] * g_i).astype(BF16)
                wgrad[j, kx, :, 1024 + b * 256 : 1024 + (b + 1) * 256] = (
                    rep[re] * g_i - rep[im] * g_r
                ).astype(BF16)

    def y_inverse(a, j):
        first = dot(y_inv(), mix[0]).astype(BF16)
        ns[a, j, :, : 2 * YL, :] = first.reshape(narrow, 2 * YL, 128)
        both = dot(y_inv_split(), mix[1])
        half = narrow * YL
        last = jnp.where(lane < 2, both[:half], shift(both[half:], 2)).astype(BF16)
        ns[a, j, :, 2 * YL :, :] = last.reshape(narrow, YL, 128)
        send_narrow(a, j)

    def x_inverse(a, j):
        wait_all(nr, a, j, nr_sem, narrow)
        t1[...] = nr[a, j, :, : 2 * YL, :].reshape(narrow * 2 * YL, 128).astype(F32)
        t1_last[...] = nr[a, j, :, 2 * YL :, :].reshape(narrow * YL, 128).astype(F32)
        for yb in range(4):
            lanes = slice(yb * 128, (yb + 1) * 128)
            ys = [4 * yb + g for g in range(4)]
            loaded = [
                [t1[pl.ds(ri * YL + y, narrow, stride=2 * YL), :] for y in ys] for ri in range(2)
            ]
            last = [t1_last[pl.ds(y, narrow, stride=YL), :] for y in ys]
            for kx in range(KXL):
                both = []
                for ri in range(2):
                    source = loaded[ri] if kx < 4 else last
                    s = kx if kx < 4 else ri * 2 + kx - 4
                    both.append(pick([shift(source[g], g - s) for g in range(4)]))
                t2[kx * 2 * narrow : (kx + 1) * 2 * narrow, lanes] = jnp.concatenate(
                    both, axis=0
                ).astype(BF16)
        ws[a, j] = dot(x_inv(), t2[...]).astype(BF16).reshape(wide, 2 * XL, cells)
        send_wide(a, j)

    def through_modes(back):
        @pl.loop(0, KL + 2)
        def _(t):
            @pl.when(t < KL)
            def _():
                x_forward(2 * back, t)

            @pl.when((t >= 1) & (t <= KL))
            def _():
                y_forward(2 * back, t - 1, back)
                mix_back(t - 1) if back else mix_forward(t - 1)
                y_inverse(2 * back + 1, t - 1)

            @pl.when(t >= 2)
            def _():
                x_inverse(2 * back + 1, t - 2)

    def depth_in(a):
        @pl.loop(0, KL)
        def _(j):
            wait_all(wr, a, j, wr_sem, wide)
            out = dot(wr[a, j].reshape(rows_j, cells), perm_t[...])
            for b in range(4):
                block = out[:, b * 128 : (b + 1) * 128]
                if a == 1:
                    zi[b, part(j), :] = block
                else:
                    back_rows[b, part(j), :] = block.astype(BF16)

    def pointwise(matrix, source):
        @pl.loop(0, XL)
        def _(x):
            near[x] = dot(matrix[...], source[:, x].reshape(cells, NZ))

    loads[0].wait()
    loads[1].wait()
    for x in range(XL):
        plane = field[:, x].reshape(cells, NZ)
        for b in range(4):
            depth(x, b, plane[b * 128 : (b + 1) * 128])

    pl.semaphore_wait(barrier, wide + narrow - 2)
    depth_out(0)

    loads[2].wait()
    loads[3].wait()
    perm_t[...] = ones_where(((row >> 5) == (col & 15)) & ((row & 31) == (col >> 4)))
    spread_row = lax.broadcasted_iota(jnp.int32, (cells, C), 0)
    spread_col = lax.broadcasted_iota(jnp.int32, (cells, C), 1)
    spread = ones_where((spread_row >> 4) == spread_col)
    same_y = (row & 15) == (col & 15)
    behind = dot(dot(spread, pw[...]).astype(BF16), spread, ((1,), (1,)))
    pw_back[...] = jnp.where(same_y, behind, 0.0).astype(BF16)
    ahead = dot(dot(spread, pw[...], ((1,), (1,))).astype(BF16), spread, ((1,), (1,)))
    pw_fwd[...] = jnp.where(same_y, ahead, 0.0).astype(BF16)
    r_row = lax.broadcasted_iota(jnp.int32, (128, 1024), 0)
    r_col = lax.broadcasted_iota(jnp.int32, (128, 1024), 1)
    repeat[...] = ones_where(r_row == (r_col >> 5))
    t_row = lax.broadcasted_iota(jnp.int32, (128, 128), 0)
    t_col = lax.broadcasted_iota(jnp.int32, (128, 128), 1)
    tile[...] = ones_where(t_row == (t_col & 31))
    g_row = lax.broadcasted_iota(jnp.int32, (1024, 128), 0)
    g_col = lax.broadcasted_iota(jnp.int32, (1024, 128), 1)
    group_sum[...] = ones_where((g_row >> 5) == (g_col & 31))
    pointwise(pw_fwd, field)
    loads[4].wait()
    loads[5].wait()

    through_modes(0)
    depth_in(1)

    root = 0.7978845608028654

    @pl.loop(0, 4)
    def _(b):
        rows = pl.ds(pl.multiple_of(b * 128, 128), 128)
        group = pl.ds(b * 8, 8)
        for x in range(XL):
            block = zi[b, pl.ds(x, kk, stride=XL), :].astype(BF16)
            t = dot(block, z_fwd(), ((0,), (0,))) + near[x, rows, :]
            square = t * t
            th = jnp.tanh(root * t * (1.0 + 0.044715 * square))
            half = 0.5 + 0.5 * th
            act[group, x] = (t * half).astype(BF16).reshape(8, YL, NZ)
            grad = half + (0.5 * root) * t * (1.0 - th * th) * (1.0 + 0.134145 * square)
            up = cot[group, x].reshape(128, NZ).astype(F32)
            block = (up * grad).astype(BF16)
            slope[group, x] = block.reshape(8, YL, NZ)
            depth(x, b, block)

    depth_out(2)
    stores = [
        pltpu.make_async_copy(src, dst, store_sem.at[i])
        for i, (src, dst) in enumerate(
            ((act, act_hbm), (near, near_hbm), (wgrad, wgrad_hbm), (back_rows, back_hbm))
        )
    ]
    stores[0].start()
    pointwise(pw_back, slope)
    stores[1].start()
    through_modes(1)
    pl.loop(0, KL)(weight_gradient)
    stores[2].start()
    depth_in(3)
    stores[3].start()

    @pl.loop(0, 4)
    def _(a):
        @pl.loop(0, KL)
        def _(j):
            wait_all(ws, a, j, ws_sem, wide)
            wait_all(ns, a, j, ns_sem, narrow)

    for store in stores:
        store.wait()


def finish(
    kk, act_in, wgrad_in, back_hbm, near_hbm, table_hbm,
    act_hbm, wgrad_hbm, fgrad_hbm,
    back, near, table, zi, fgrad, sem,
):
    stores = [
        pltpu.make_async_copy(act_in, act_hbm, sem.at[0]),
        pltpu.make_async_copy(wgrad_in, wgrad_hbm, sem.at[1]),
    ]
    load_table = pltpu.make_async_copy(table_hbm.at[pl.ds(0, kk)], table, sem.at[2])
    load_table.start()
    loads = []
    for b in range(4):
        rows = pl.ds(b * 128, 128)
        loads.append(
            (
                pltpu.make_async_copy(back_hbm.at[b], back.at[b], sem.at[3 + b]),
                pltpu.make_async_copy(near_hbm.at[:, rows], near.at[:, rows], sem.at[7 + b]),
            )
        )
        for load in loads[-1]:
            load.start()
    for store in stores:
        store.start()
    load_table.wait()
    for b in range(4):
        for load in loads[b]:
            load.wait()
        zi[b] = back[b].astype(F32)
        for x in range(XL):
            block = zi[b, pl.ds(x, kk, stride=XL), :].astype(BF16)
            t = dot(block, table[...], ((0,), (0,))) + near[x, b * 128 : (b + 1) * 128, :]
            fgrad[b * 8 : (b + 1) * 8, x] = t.astype(BF16).reshape(8, YL, NZ)
        group = pl.ds(b * 8, 8)
        stores.append(pltpu.make_async_copy(fgrad.at[group], fgrad_hbm.at[group], sem.at[11 + b]))
        stores[-1].start()
    for store in stores:
        store.wait()


def on_device(wide, narrow, field, weight, pw, cot):
    ky = weight.shape[2]
    total = float(XL * wide * YL * narrow * NZ)
    places, packed = tables(wide, narrow, ky)
    table = jnp.asarray(packed)
    cells = C * YL
    kk = KL * wide * 2
    modes = KXL * 2 * ky
    hbm = pl.BlockSpec(memory_space=pl.ANY)
    grid_like = jax.ShapeDtypeStruct(field.shape, BF16)
    weight_like = jax.ShapeDtypeStruct(weight.shape, BF16)
    parts = pl.pallas_call(
        functools.partial(kernel, wide, narrow, ky, total, places),
        out_shape=(
            grid_like,
            weight_like,
            jax.ShapeDtypeStruct((4, kk * XL, 128), BF16),
            jax.ShapeDtypeStruct((XL, cells, NZ), F32),
        ),
        in_specs=[hbm] * 5,
        out_specs=(hbm,) * 4,
        scratch_shapes=[
            pltpu.VMEM(table.shape, BF16),
            pltpu.VMEM(field.shape, BF16),
            pltpu.VMEM(cot.shape, BF16),
            pltpu.VMEM(weight.shape, BF16),
            pltpu.VMEM(pw.shape, BF16),
            pltpu.VMEM(field.shape, BF16),
            pltpu.VMEM(weight.shape, BF16),
            pltpu.VMEM((4, kk * XL, 128), F32),
            pltpu.VMEM((XL, cells, NZ), F32),
            pltpu.VMEM((4, kk * XL, 128), BF16),
            pltpu.VMEM((4, kk * XL, 128), F32),
            pltpu.VMEM(field.shape, BF16),
            pltpu.VMEM((2, KL, modes, 128), BF16),
            pltpu.VMEM((modes, 128), F32),
            pltpu.VMEM((modes, 1024), BF16),
            pltpu.VMEM((2, 2 * ky, 128), BF16),
            pltpu.VMEM((narrow * 2 * YL, 128), F32),
            pltpu.VMEM((narrow * YL, 128), F32),
            pltpu.VMEM((KXL * narrow * 2, cells), BF16),
            pltpu.VMEM((cells, cells), BF16),
            pltpu.VMEM((cells, cells), BF16),
            pltpu.VMEM((cells, cells), BF16),
            pltpu.VMEM((cells, cells), BF16),
            pltpu.VMEM((128, 1024), BF16),
            pltpu.VMEM((128, 128), BF16),
            pltpu.VMEM((1024, 128), BF16),
            pltpu.VMEM((4, KL, wide, 2 * XL, cells), BF16),
            pltpu.VMEM((4, KL, wide, 2 * XL, cells), BF16),
            pltpu.VMEM((4, KL, narrow, 3 * YL, 128), BF16),
            pltpu.VMEM((4, KL, narrow, 3 * YL, 128), BF16),
            pltpu.SemaphoreType.DMA((4, KL)),
            pltpu.SemaphoreType.DMA((4, KL)),
            pltpu.SemaphoreType.DMA((4, KL)),
            pltpu.SemaphoreType.DMA((4, KL)),
            pltpu.SemaphoreType.DMA((6,)),
            pltpu.SemaphoreType.DMA((4,)),
        ],
        compiler_params=pltpu.CompilerParams(
            collective_id=0, has_side_effects=True, vmem_limit_bytes=VMEM_BYTES
        ),
        name="spectral_layer",
    )(field, cot, weight, pw, table)
    act, wgrad, fgrad = pl.pallas_call(
        functools.partial(finish, kk),
        out_shape=(grid_like, weight_like, grid_like),
        in_specs=[hbm] * 5,
        out_specs=(hbm,) * 3,
        scratch_shapes=[
            pltpu.VMEM((4, kk * XL, 128), BF16),
            pltpu.VMEM((XL, cells, NZ), F32),
            pltpu.VMEM((kk, NZ), BF16),
            pltpu.VMEM((4, kk * XL, 128), F32),
            pltpu.VMEM(field.shape, BF16),
            pltpu.SemaphoreType.DMA((15,)),
        ],
        compiler_params=pltpu.CompilerParams(vmem_limit_bytes=VMEM_BYTES),
        name="field_gradient",
    )(*parts, table)
    return act, fgrad, wgrad


def solution(mesh):
    wide, narrow = mesh.shape["wide"], mesh.shape["narrow"]
    return jax.shard_map(
        functools.partial(on_device, wide, narrow),
        mesh=mesh,
        in_specs=(
            P(None, "wide", "narrow", None),
            P("wide", "narrow", None, None),
            P(),
            P(None, "wide", "narrow", None),
        ),
        out_specs=(
            P(None, "wide", "narrow", None),
            P(None, "wide", "narrow", None),
            P("wide", "narrow", None, None),
        ),
        check_vma=False,
    )
```

time: 99.7 us -> 222 us (2.23)
  Pallas kernels: 86.9 us -> 221 us
  local copies, waits for them, and re-layouts: 11.7 us -> 0 us
    pallas_call x1 -> x2, Pallas kernels: 86.9 us -> 221 us  [the longest x1 140 us: on_device(): pl.pallas_call(functools.partial(finish, kk), out_shape=(grid_like, weigh...]
    unnamed x21 -> x0, local copies, waits for them, and re-layouts: 11.7 us -> none
where the time goes in v1:
time: 222 us
  Pallas kernels  221 us (100%)
    pallas_call x1, Pallas kernels, on_device(): pl.pallas_call(functools.partial(finish, kk), out_shape=(grid_like, weigh...  140 us
    pallas_call x1, Pallas kernels, on_device(): pl.pallas_call(functools.partial(kernel, wide, narrow, ky, total, places)...  81.1 us

profile of v1, /device:TPU:1, one launch (start us, length us, event | category | flops | bytes accessed | tf_op | source)
XLA Modules:
  0.0 221.9 jit_solution(13436340411768069199)
XLA Ops:
  0.6 81.1 %spectral_layer.1 = (bf16[32,8,16,128]{3,2,1,0:T(8,128)(2,1)}, bf16[3,6,48,2048]{3,2,1,0:T(8,128)(2,1)}, bf16[4,768,128]{2,1,0:T(8,128)(2,1)}, f32[8,512,128]{2,1,0:T(8,128)}) custom-call(bf16[32,8,16,128]{3,2,1,0:T(8,128)(2,1)} %field_hbm.1, bf16[32,8,16,128]{3,2,1,0:T(8,128)(2,1)} %cot_hbm.1, bf16[3,6,48,2048]{3,2,1,0:T(8,128)(2,1)} %weight_hbm.1, ...), custom_call_target="tpu_custom_call" | custom-call | tf_op jit(solution)/shard_map/spectral_layer/pallas_call | solution.py:486
  81.7 140.2 %field_gradient.1 = (bf16[32,8,16,128]{3,2,1,0:T(8,128)(2,1)}, bf16[3,6,48,2048]{3,2,1,0:T(8,128)(2,1)}, bf16[32,8,16,128]{3,2,1,0:T(8,128)(2,1)}) custom-call(bf16[32,8,16,128]{3,2,1,0:T(8,128)(2,1)} %get-tuple-element.10.act_in, bf16[3,6,48,2048]{3,2,1,0:T(8,128)(2,1)} %get-tuple-element.11.wgrad_in, bf16[4,768,128]{2,1,0:T(8,128)(2,1)} %get-tuple-element.12.back_hbm, ...), custom_call_target="tpu_custom_call" | custom-call | tf_op jit(solution)/shard_map/field_gradient/pallas_call | solution.py:539

commit v2 on v1

--- a/solution.py
+++ b/solution.py
@@ -124,10 +124,13 @@
 
     barrier = pltpu.get_barrier_semaphore()
 
-    @pl.loop(1, wide)
+    half = narrow // 2
+    flip = lax.rem(n + half, narrow)
+
+    @pl.loop(0, wide)
     def _(d):
         pl.semaphore_signal(
-            barrier, inc=1, device_id={"wide": lax.rem(w + d, wide)}, device_id_type=MESH
+            barrier, inc=1, device_id={"wide": d, "narrow": flip}, device_id_type=MESH
         )
 
     @pl.loop(1, narrow)
@@ -156,29 +159,36 @@
         out = dot(z_fwd(), block, ((1,), (1,)))
         zs[b, pl.ds(x, kk, stride=XL), :] = out
 
-    def send(axis, count, me, src, dst, send_sem, recv_sem, a, j):
-        dst[a, j, me] = src[a, j, me]
-
-        @pl.loop(1, count)
+    def send_wide(a, j):
+        @pl.loop(0, wide)
         def _(d):
-            to = lax.rem(me + d, count)
+            to = lax.rem(w + d, wide)
             pltpu.make_async_remote_copy(
-                src_ref=src.at[a, j, to],
-                dst_ref=dst.at[a, j, me],
-                send_sem=send_sem.at[a, j],
-                recv_sem=recv_sem.at[a, j],
-                device_id={axis: to},
+                src_ref=ws.at[a, j, to],
+                dst_ref=wr.at[a, j, w],
+                send_sem=ws_sem.at[a, j],
+                recv_sem=wr_sem.at[a, j],
+                device_id={"wide": to, "narrow": flip},
                 device_id_type=MESH,
             ).start()
 
-    def send_wide(a, j):
-        send("wide", wide, w, ws, wr, ws_sem, wr_sem, a, j)
-
-    def send_narrow(a, j):
-        send("narrow", narrow, n, ns, nr, ns_sem, nr_sem, a, j)
+    def send_narrow(a, j, take, slot):
+        nr[a, j, slot] = ns[a, j, take(n)]
+
+        @pl.loop(1, narrow)
+        def _(d):
+            to = lax.rem(n + d, narrow)
+            pltpu.make_async_remote_copy(
+                src_ref=ns.at[a, j, take(to)],
+                dst_ref=nr.at[a, j, slot],
+                send_sem=ns_sem.at[a, j],
+                recv_sem=nr_sem.at[a, j],
+                device_id={"narrow": to},
+                device_id_type=MESH,
+            ).start()
 
     def wait_all(buffer, a, j, sem, count):
-        ref = buffer.at[a, j, pl.ds(0, count - 1)]
+        ref = buffer.at[a, j, pl.ds(0, count)]
         pltpu.make_async_copy(ref, ref, sem.at[a, j]).wait()
 
     def part(j):
@@ -210,10 +220,10 @@
             )
         ns[a, j, :, : 2 * YL, :] = t1[...].astype(BF16).reshape(narrow, 2 * YL, 128)
         ns[a, j, :, 2 * YL :, :] = t1_last[...].astype(BF16).reshape(narrow, YL, 128)
-        send_narrow(a, j)
+        send_narrow(a, j, lambda to: to, flip)
 
     def y_forward(a, j, which):
-        wait_all(nr, a, j, nr_sem, narrow)
+        wait_all(nr, a, j, nr_sem, narrow - 1)
         first = dot(y_fwd(), nr[a, j, :, : 2 * YL, :].reshape(narrow * 2 * YL, 128))
         both = dot(y_fwd_split(), nr[a, j, :, 2 * YL :, :].reshape(narrow * YL, 128))
         last = both[: 2 * ky] + shift(both[2 * ky :], 2)
@@ -287,13 +297,13 @@
         first = dot(y_inv(), mix[0]).astype(BF16)
         ns[a, j, :, : 2 * YL, :] = first.reshape(narrow, 2 * YL, 128)
         both = dot(y_inv_split(), mix[1])
-        half = narrow * YL
-        last = jnp.where(lane < 2, both[:half], shift(both[half:], 2)).astype(BF16)
+        split = narrow * YL
+        last = jnp.where(lane < 2, both[:split], shift(both[split:], 2)).astype(BF16)
         ns[a, j, :, 2 * YL :, :] = last.reshape(narrow, YL, 128)
-        send_narrow(a, j)
+        send_narrow(a, j, lambda to: lax.rem(to + half, narrow), n)
 
     def x_inverse(a, j):
-        wait_all(nr, a, j, nr_sem, narrow)
+        wait_all(nr, a, j, nr_sem, narrow - 1)
         t1[...] = nr[a, j, :, : 2 * YL, :].reshape(narrow * 2 * YL, 128).astype(F32)
         t1_last[...] = nr[a, j, :, 2 * YL :, :].reshape(narrow * YL, 128).astype(F32)
         for yb in range(4):
@@ -356,7 +366,7 @@
         for b in range(4):
             depth(x, b, plane[b * 128 : (b + 1) * 128])
 
-    pl.semaphore_wait(barrier, wide + narrow - 2)
+    pl.semaphore_wait(barrier, wide + narrow - 1)
     depth_out(0)
 
     loads[2].wait()
@@ -397,9 +407,9 @@
             t = dot(block, z_fwd(), ((0,), (0,))) + near[x, rows, :]
             square = t * t
             th = jnp.tanh(root * t * (1.0 + 0.044715 * square))
-            half = 0.5 + 0.5 * th
-            act[group, x] = (t * half).astype(BF16).reshape(8, YL, NZ)
-            grad = half + (0.5 * root) * t * (1.0 - th * th) * (1.0 + 0.134145 * square)
+            gate = 0.5 + 0.5 * th
+            act[group, x] = (t * gate).astype(BF16).reshape(8, YL, NZ)
+            grad = gate + (0.5 * root) * t * (1.0 - th * th) * (1.0 + 0.134145 * square)
             up = cot[group, x].reshape(128, NZ).astype(F32)
             block = (up * grad).astype(BF16)
             slope[group, x] = block.reshape(8, YL, NZ)
@@ -426,7 +436,7 @@
         @pl.loop(0, KL)
         def _(j):
             wait_all(ws, a, j, ws_sem, wide)
-            wait_all(ns, a, j, ns_sem, narrow)
+            wait_all(ns, a, j, ns_sem, narrow - 1)
 
     for store in stores:
         store.wait()
@@ -435,27 +445,32 @@
 def finish(
     kk, act_in, wgrad_in, back_hbm, near_hbm, table_hbm,
     act_hbm, wgrad_hbm, fgrad_hbm,
-    back, near, table, zi, fgrad, sem,
+    back, near, table, zi, fgrad, act, wgrad, sem,
 ):
-    stores = [
-        pltpu.make_async_copy(act_in, act_hbm, sem.at[0]),
-        pltpu.make_async_copy(wgrad_in, wgrad_hbm, sem.at[1]),
-    ]
-    load_table = pltpu.make_async_copy(table_hbm.at[pl.ds(0, kk)], table, sem.at[2])
+    load_table = pltpu.make_async_copy(table_hbm.at[pl.ds(0, kk)], table, sem.at[0])
     load_table.start()
-    loads = []
+    loads, passed, stores = [], [], []
     for b in range(4):
         rows = pl.ds(b * 128, 128)
         loads.append(
             (
-                pltpu.make_async_copy(back_hbm.at[b], back.at[b], sem.at[3 + b]),
-                pltpu.make_async_copy(near_hbm.at[:, rows], near.at[:, rows], sem.at[7 + b]),
+                pltpu.make_async_copy(back_hbm.at[b], back.at[b], sem.at[1 + b]),
+                pltpu.make_async_copy(near_hbm.at[:, rows], near.at[:, rows], sem.at[5 + b]),
             )
         )
         for load in loads[-1]:
             load.start()
-    for store in stores:
-        store.start()
+    whole = [(act_in, act, act_hbm)] + [
+        (wgrad_in.at[j], wgrad.at[j], wgrad_hbm.at[j]) for j in range(KL)
+    ]
+    for i, (src, held, dst) in enumerate(whole):
+        passed.append(
+            (
+                pltpu.make_async_copy(src, held, sem.at[9 + i]),
+                pltpu.make_async_copy(held, dst, sem.at[13 + i]),
+            )
+        )
+        passed[-1][0].start()
     load_table.wait()
     for b in range(4):
         for load in loads[b]:
@@ -466,8 +481,11 @@
             t = dot(block, table[...], ((0,), (0,))) + near[x, b * 128 : (b + 1) * 128, :]
             fgrad[b * 8 : (b + 1) * 8, x] = t.astype(BF16).reshape(8, YL, NZ)
         group = pl.ds(b * 8, 8)
-        stores.append(pltpu.make_async_copy(fgrad.at[group], fgrad_hbm.at[group], sem.at[11 + b]))
+        stores.append(pltpu.make_async_copy(fgrad.at[group], fgrad_hbm.at[group], sem.at[17 + b]))
         stores[-1].start()
+        passed[b][0].wait()
+        passed[b][1].start()
+        stores.append(passed[b][1])
     for store in stores:
         store.wait()
 
@@ -547,7 +565,9 @@
             pltpu.VMEM((kk, NZ), BF16),
             pltpu.VMEM((4, kk * XL, 128), F32),
             pltpu.VMEM(field.shape, BF16),
-            pltpu.SemaphoreType.DMA((15,)),
+            pltpu.VMEM(field.shape, BF16),
+            pltpu.VMEM(weight.shape, BF16),
+            pltpu.SemaphoreType.DMA((21,)),
         ],
         compiler_params=pltpu.CompilerParams(vmem_limit_bytes=VMEM_BYTES),
         name="field_gradient",

time: 222 us -> 85.1 us (0.38)
  Pallas kernels: 221 us -> 84.3 us
    pallas_call x1, Pallas kernels: 140 us -> 4.96 us  [on_device(): pl.pallas_call(functools.partial(finish, kk), out_shape=(grid_like, weigh...]
where the time goes in v2:
time: 85.1 us; the launch traced here: 85 us
  Pallas kernels  84.3 us (99%)
    pallas_call x1, Pallas kernels, on_device(): pl.pallas_call(functools.partial(kernel, wide, narrow, ky, total, places)...  79.4 us
    pallas_call x1, Pallas kernels, on_device(): pl.pallas_call(functools.partial(finish, kk), out_shape=(grid_like, weigh...  4.96 us

profile of v2, /device:TPU:1, one launch (start us, length us, event | category | flops | bytes accessed | tf_op | source)
XLA Modules:
  0.0 85.0 jit_solution(17448099041412185402)
XLA Ops:
  0.6 79.4 %spectral_layer.1 = (bf16[32,8,16,128]{3,2,1,0:T(8,128)(2,1)}, bf16[3,6,48,2048]{3,2,1,0:T(8,128)(2,1)}, bf16[4,768,128]{2,1,0:T(8,128)(2,1)}, f32[8,512,128]{2,1,0:T(8,128)}) custom-call(bf16[32,8,16,128]{3,2,1,0:T(8,128)(2,1)} %field_hbm.1, bf16[32,8,16,128]{3,2,1,0:T(8,128)(2,1)} %cot_hbm.1, bf16[3,6,48,2048]{3,2,1,0:T(8,128)(2,1)} %weight_hbm.1, ...), custom_call_target="tpu_custom_call" | custom-call | tf_op jit(solution)/shard_map/spectral_layer/pallas_call | solution.py:504
  80.0 5.0 %field_gradient.1 = (bf16[32,8,16,128]{3,2,1,0:T(8,128)(2,1)}, bf16[3,6,48,2048]{3,2,1,0:T(8,128)(2,1)}, bf16[32,8,16,128]{3,2,1,0:T(8,128)(2,1)}) custom-call(bf16[32,8,16,128]{3,2,1,0:T(8,128)(2,1)} %get-tuple-element.10.act_in, bf16[3,6,48,2048]{3,2,1,0:T(8,128)(2,1)} %get-tuple-element.11.wgrad_in, bf16[4,768,128]{2,1,0:T(8,128)(2,1)} %get-tuple-element.12.back_hbm, ...), custom_call_target="tpu_custom_call" | custom-call | tf_op jit(solution)/shard_map/field_gradient/pallas_call | solution.py:557

commit v3 on v2

--- a/solution.py
+++ b/solution.py
@@ -14,6 +14,7 @@
 YL = 16
 KXL = 6
 KL = 3
+HALVES = 2
 NZ = 128
 VMEM_BYTES = 64 * 1024 * 1024
 MESH = pl.DeviceIdType.MESH
@@ -39,12 +40,13 @@
     cx, sx = angles(nx, kx, True)
     cy, sy = angles(ny, ky, True)
     cz, sz = angles(NZ, kz, False)
-    z_rows = np.stack([cz, -sz], axis=-1).reshape(NZ, wide, KL, 2)
-    z_fwd = z_rows.transpose(2, 1, 3, 0).reshape(KL * wide * 2, NZ)
+    v = wide // HALVES
+    z_rows = np.stack([cz, -sz], axis=-1).reshape(NZ, HALVES, v, KL, 2)
+    z_fwd = z_rows.transpose(3, 2, 1, 4, 0).reshape(KL * wide * 2, NZ)
     fwd = lambda c, s: np.stack([np.stack([c, s]), np.stack([-s, c])])
     inv = lambda c, s: np.stack([np.stack([c, -s]), np.stack([s, c])])
-    fx = fwd(cx, sx).reshape(2, 2, wide, XL, narrow, KXL)
-    x_fwd = fx.transpose(5, 0, 4, 2, 1, 3).reshape(KXL * 2 * narrow, wide * 2 * XL)
+    fx = fwd(cx, sx).reshape(2, 2, HALVES, v, XL, narrow, KXL)
+    x_fwd = fx.transpose(2, 6, 0, 5, 3, 1, 4).reshape(HALVES * KXL * 2 * narrow, v * 2 * XL)
     ix = inv(cx, sx).reshape(2, 2, wide, XL, narrow, KXL)
     x_inv = ix.transpose(2, 0, 3, 5, 1, 4).reshape(wide * 2 * XL, KXL * 2 * narrow)
     fy = fwd(cy, sy).reshape(2, 2, narrow, YL, ky)
@@ -122,22 +124,24 @@
     for load in loads:
         load.start()
 
+    side = wide // HALVES
+    h, v = w // side, lax.rem(w, side)
+    plane = HALVES * narrow
+    here = h * narrow + n
+
     barrier = pltpu.get_barrier_semaphore()
 
-    half = narrow // 2
-    flip = lax.rem(n + half, narrow)
-
-    @pl.loop(0, wide)
-    def _(d):
-        pl.semaphore_signal(
-            barrier, inc=1, device_id={"wide": d, "narrow": flip}, device_id_type=MESH
-        )
-
-    @pl.loop(1, narrow)
-    def _(d):
-        pl.semaphore_signal(
-            barrier, inc=1, device_id={"narrow": lax.rem(n + d, narrow)}, device_id_type=MESH
-        )
+    def along(d):
+        to = lax.rem(v + d, side)
+        return to, {"wide": h * side + to}
+
+    def across(d):
+        to = lax.rem(here + d, plane)
+        return to, {"wide": to // narrow * side + v, "narrow": lax.rem(to, narrow)}
+
+    for count, peer in ((side, along), (plane, across)):
+        for d in range(1, count):
+            pl.semaphore_signal(barrier, inc=1, device_id=peer(d)[1], device_id_type=MESH)
 
     row = lax.broadcasted_iota(jnp.int32, (cells, cells), 0)
     col = lax.broadcasted_iota(jnp.int32, (cells, cells), 1)
@@ -159,33 +163,25 @@
         out = dot(z_fwd(), block, ((1,), (1,)))
         zs[b, pl.ds(x, kk, stride=XL), :] = out
 
-    def send_wide(a, j):
-        @pl.loop(0, wide)
-        def _(d):
-            to = lax.rem(w + d, wide)
+    def send(peer, count, src, dst, slot, send_sem, recv_sem, take=lambda to: to):
+        for d in range(1, count):
+            to, device = peer(d)
             pltpu.make_async_remote_copy(
-                src_ref=ws.at[a, j, to],
-                dst_ref=wr.at[a, j, w],
-                send_sem=ws_sem.at[a, j],
-                recv_sem=wr_sem.at[a, j],
-                device_id={"wide": to, "narrow": flip},
+                src_ref=src.at[take(to)],
+                dst_ref=dst.at[slot],
+                send_sem=send_sem,
+                recv_sem=recv_sem,
+                device_id=device,
                 device_id_type=MESH,
             ).start()
 
-    def send_narrow(a, j, take, slot):
-        nr[a, j, slot] = ns[a, j, take(n)]
-
-        @pl.loop(1, narrow)
-        def _(d):
-            to = lax.rem(n + d, narrow)
-            pltpu.make_async_remote_copy(
-                src_ref=ns.at[a, j, take(to)],
-                dst_ref=nr.at[a, j, slot],
-                send_sem=ns_sem.at[a, j],
-                recv_sem=nr_sem.at[a, j],
-                device_id={"narrow": to},
-                device_id_type=MESH,
-            ).start()
+    def send_wide(a, j):
+        wr[a, j, v] = ws[a, j, v]
+        send(along, side, ws.at[a, j], wr.at[a, j], v, ws_sem.at[a, j], wr_sem.at[a, j])
+
+    def send_narrow(a, j, take):
+        nr[a, j, here] = ns[a, j, take(here)]
+        send(across, plane, ns.at[a, j], nr.at[a, j], here, ns_sem.at[a, j], nr_sem.at[a, j], take)
 
     def wait_all(buffer, a, j, sem, count):
         ref = buffer.at[a, j, pl.ds(0, count)]
@@ -198,34 +194,43 @@
         @pl.loop(0, KL)
         def _(j):
             block = jnp.concatenate([zs[b, part(j), :].astype(BF16) for b in range(4)], axis=1)
-            ws[a, j] = dot(block, perm[...]).astype(BF16).reshape(wide, 2 * XL, cells)
+            ws[a, j] = dot(block, perm[...]).astype(BF16).reshape(side, HALVES * 2 * XL, cells)
             send_wide(a, j)
 
     def x_forward(a, j):
-        wait_all(wr, a, j, wr_sem, wide)
-        out = dot(x_fwd(), wr[a, j].reshape(rows_j, cells))
-        for y in range(YL):
-            yb, g = y // 4, y % 4
-
-            def piece(kx, ri):
-                first = (kx * 2 + ri) * narrow
-                return out[first : first + narrow, yb * 128 : (yb + 1) * 128]
-
-            for ri in range(2):
-                t1[pl.ds(ri * YL + y, narrow, stride=2 * YL), :] = pick(
-                    [shift(piece(s, ri), s - g) for s in range(4)]
+        wait_all(wr, a, j, wr_sem, side - 1)
+        first, rows, columns = places[1]
+        rows = rows // HALVES
+        matrix = table[pl.ds(first + h * rows, rows), :columns]
+        for to_h in range(HALVES):
+            part_rows = slice(to_h * 2 * XL, (to_h + 1) * 2 * XL)
+            out = dot(matrix, wr[a, j, :, part_rows, :].reshape(side * 2 * XL, cells))
+            for y in range(YL):
+                yb, g = y // 4, y % 4
+
+                def piece(kx, ri):
+                    first = (kx * 2 + ri) * narrow
+                    return out[first : first + narrow, yb * 128 : (yb + 1) * 128]
+
+                for ri in range(2):
+                    t1[pl.ds(ri * YL + y, narrow, stride=2 * YL), :] = pick(
+                        [shift(piece(s, ri), s - g) for s in range(4)]
+                    )
+                t1_last[pl.ds(y, narrow, stride=YL), :] = pick(
+                    [shift(piece(4 + s % 2, s // 2), s - g) for s in range(4)]
                 )
-            t1_last[pl.ds(y, narrow, stride=YL), :] = pick(
-                [shift(piece(4 + s % 2, s // 2), s - g) for s in range(4)]
-            )
-        ns[a, j, :, : 2 * YL, :] = t1[...].astype(BF16).reshape(narrow, 2 * YL, 128)
-        ns[a, j, :, 2 * YL :, :] = t1_last[...].astype(BF16).reshape(narrow, YL, 128)
-        send_narrow(a, j, lambda to: to, flip)
+            owners = slice(to_h * narrow, (to_h + 1) * narrow)
+            ns[a, j, owners, : 2 * YL, :] = t1[...].astype(BF16).reshape(narrow, 2 * YL, 128)
+            ns[a, j, owners, 2 * YL :, :] = t1_last[...].astype(BF16).reshape(narrow, YL, 128)
+        send_narrow(a, j, lambda to: to)
 
     def y_forward(a, j, which):
-        wait_all(nr, a, j, nr_sem, narrow - 1)
-        first = dot(y_fwd(), nr[a, j, :, : 2 * YL, :].reshape(narrow * 2 * YL, 128))
-        both = dot(y_fwd_split(), nr[a, j, :, 2 * YL :, :].reshape(narrow * YL, 128))
+        wait_all(nr, a, j, nr_sem, plane - 1)
+        halves = [slice(i * narrow, (i + 1) * narrow) for i in range(HALVES)]
+        first, both = (
+            sum(dot(matrix, nr[a, j, i, lines, :].reshape(-1, 128)) for i in halves)
+            for matrix, lines in ((y_fwd(), slice(0, 2 * YL)), (y_fwd_split(), slice(2 * YL, None)))
+        )
         last = both[: 2 * ky] + shift(both[2 * ky :], 2)
         for kx in range(KXL):
             source = first if kx < 4 else last
@@ -295,34 +300,41 @@
 
     def y_inverse(a, j):
         first = dot(y_inv(), mix[0]).astype(BF16)
-        ns[a, j, :, : 2 * YL, :] = first.reshape(narrow, 2 * YL, 128)
+        ns[a, j, :narrow, : 2 * YL, :] = first.reshape(narrow, 2 * YL, 128)
         both = dot(y_inv_split(), mix[1])
         split = narrow * YL
         last = jnp.where(lane < 2, both[:split], shift(both[split:], 2)).astype(BF16)
-        ns[a, j, :, 2 * YL :, :] = last.reshape(narrow, YL, 128)
-        send_narrow(a, j, lambda to: lax.rem(to + half, narrow), n)
+        ns[a, j, :narrow, 2 * YL :, :] = last.reshape(narrow, YL, 128)
+        send_narrow(a, j, lambda to: lax.rem(to, narrow))
 
     def x_inverse(a, j):
-        wait_all(nr, a, j, nr_sem, narrow - 1)
-        t1[...] = nr[a, j, :, : 2 * YL, :].reshape(narrow * 2 * YL, 128).astype(F32)
-        t1_last[...] = nr[a, j, :, 2 * YL :, :].reshape(narrow * YL, 128).astype(F32)
-        for yb in range(4):
-            lanes = slice(yb * 128, (yb + 1) * 128)
-            ys = [4 * yb + g for g in range(4)]
-            loaded = [
-                [t1[pl.ds(ri * YL + y, narrow, stride=2 * YL), :] for y in ys] for ri in range(2)
-            ]
-            last = [t1_last[pl.ds(y, narrow, stride=YL), :] for y in ys]
-            for kx in range(KXL):
-                both = []
-                for ri in range(2):
-                    source = loaded[ri] if kx < 4 else last
-                    s = kx if kx < 4 else ri * 2 + kx - 4
-                    both.append(pick([shift(source[g], g - s) for g in range(4)]))
-                t2[kx * 2 * narrow : (kx + 1) * 2 * narrow, lanes] = jnp.concatenate(
-                    both, axis=0
-                ).astype(BF16)
-        ws[a, j] = dot(x_inv(), t2[...]).astype(BF16).reshape(wide, 2 * XL, cells)
+        wait_all(nr, a, j, nr_sem, plane - 1)
+        first, rows, columns = places[2]
+        rows = rows // HALVES
+        matrix = table[pl.ds(first + h * rows, rows), :columns]
+        for from_h in range(HALVES):
+            owners = slice(from_h * narrow, (from_h + 1) * narrow)
+            t1[...] = nr[a, j, owners, : 2 * YL, :].reshape(narrow * 2 * YL, 128).astype(F32)
+            t1_last[...] = nr[a, j, owners, 2 * YL :, :].reshape(narrow * YL, 128).astype(F32)
+            for yb in range(4):
+                lanes = slice(yb * 128, (yb + 1) * 128)
+                ys = [4 * yb + g for g in range(4)]
+                loaded = [
+                    [t1[pl.ds(ri * YL + y, narrow, stride=2 * YL), :] for y in ys] for ri in range(2)
+                ]
+                last = [t1_last[pl.ds(y, narrow, stride=YL), :] for y in ys]
+                for kx in range(KXL):
+                    both = []
+                    for ri in range(2):
+                        source = loaded[ri] if kx < 4 else last
+                        s = kx if kx < 4 else ri * 2 + kx - 4
+                        both.append(pick([shift(source[g], g - s) for g in range(4)]))
+                    t2[kx * 2 * narrow : (kx + 1) * 2 * narrow, lanes] = jnp.concatenate(
+                        both, axis=0
+                    ).astype(BF16)
+            out = dot(matrix, t2[...]).astype(BF16)
+            part_rows = slice(from_h * 2 * XL, (from_h + 1) * 2 * XL)
+            ws[a, j, :, part_rows, :] = out.reshape(side, 2 * XL, cells)
         send_wide(a, j)
 
     def through_modes(back):
@@ -345,7 +357,7 @@
     def depth_in(a):
         @pl.loop(0, KL)
         def _(j):
-            wait_all(wr, a, j, wr_sem, wide)
+            wait_all(wr, a, j, wr_sem, side - 1)
             out = dot(wr[a, j].reshape(rows_j, cells), perm_t[...])
             for b in range(4):
                 block = out[:, b * 128 : (b + 1) * 128]
@@ -362,11 +374,11 @@
     loads[0].wait()
     loads[1].wait()
     for x in range(XL):
-        plane = field[:, x].reshape(cells, NZ)
+        slab = field[:, x].reshape(cells, NZ)
         for b in range(4):
-            depth(x, b, plane[b * 128 : (b + 1) * 128])
-
-    pl.semaphore_wait(barrier, wide + narrow - 1)
+            depth(x, b, slab[b * 128 : (b + 1) * 128])
+
+    pl.semaphore_wait(barrier, side + plane - 2)
     depth_out(0)
 
     loads[2].wait()
@@ -435,8 +447,8 @@
     def _(a):
         @pl.loop(0, KL)
         def _(j):
-            wait_all(ws, a, j, ws_sem, wide)
-            wait_all(ns, a, j, ns_sem, narrow - 1)
+            wait_all(ws, a, j, ws_sem, side - 1)
+            wait_all(ns, a, j, ns_sem, plane - 1)
 
     for store in stores:
         store.wait()
@@ -498,6 +510,7 @@
     cells = C * YL
     kk = KL * wide * 2
     modes = KXL * 2 * ky
+    side, plane = wide // HALVES, narrow * HALVES
     hbm = pl.BlockSpec(memory_space=pl.ANY)
     grid_like = jax.ShapeDtypeStruct(field.shape, BF16)
     weight_like = jax.ShapeDtypeStruct(weight.shape, BF16)
@@ -538,10 +551,10 @@
             pltpu.VMEM((128, 1024), BF16),
             pltpu.VMEM((128, 128), BF16),
             pltpu.VMEM((1024, 128), BF16),
-            pltpu.VMEM((4, KL, wide, 2 * XL, cells), BF16),
-            pltpu.VMEM((4, KL, wide, 2 * XL, cells), BF16),
-            pltpu.VMEM((4, KL, narrow, 3 * YL, 128), BF16),
-            pltpu.VMEM((4, KL, narrow, 3 * YL, 128), BF16),
+            pltpu.VMEM((4, KL, side, HALVES * 2 * XL, cells), BF16),
+            pltpu.VMEM((4, KL, side, HALVES * 2 * XL, cells), BF16),
+            pltpu.VMEM((4, KL, plane, 3 * YL, 128), BF16),
+            pltpu.VMEM((4, KL, plane, 3 * YL, 128), BF16),
             pltpu.SemaphoreType.DMA((4, KL)),
             pltpu.SemaphoreType.DMA((4, KL)),
             pltpu.SemaphoreType.DMA((4, KL)),

time: 85.1 us -> 86.9 us (1.021)
  Pallas kernels: 84.3 us -> 86.2 us
    pallas_call x1, Pallas kernels: 79.4 us -> 81.2 us  [on_device(): pl.pallas_call(functools.partial(kernel, wide, narrow, ky, total, places)...]
where the time goes in v3:
time: 86.9 us; the launch traced here: 86.8 us
  Pallas kernels  86.2 us (99%)
    pallas_call x1, Pallas kernels, on_device(): pl.pallas_call(functools.partial(kernel, wide, narrow, ky, total, places)...  81.2 us
    pallas_call x1, Pallas kernels, on_device(): pl.pallas_call(functools.partial(finish, kk), out_shape=(grid_like, weigh...  4.96 us

profile of v3, /device:TPU:1, one launch (start us, length us, event | category | flops | bytes accessed | tf_op | source)
XLA Modules:
  0.0 86.8 jit_solution(16387163131579928437)
XLA Ops:
  0.6 81.2 %spectral_layer.1 = (bf16[32,8,16,128]{3,2,1,0:T(8,128)(2,1)}, bf16[3,6,48,2048]{3,2,1,0:T(8,128)(2,1)}, bf16[4,768,128]{2,1,0:T(8,128)(2,1)}, f32[8,512,128]{2,1,0:T(8,128)}) custom-call(bf16[32,8,16,128]{3,2,1,0:T(8,128)(2,1)} %field_hbm.1, bf16[32,8,16,128]{3,2,1,0:T(8,128)(2,1)} %cot_hbm.1, bf16[3,6,48,2048]{3,2,1,0:T(8,128)(2,1)} %weight_hbm.1, ...), custom_call_target="tpu_custom_call" | custom-call | tf_op jit(solution)/shard_map/spectral_layer/pallas_call | solution.py:517
  81.9 5.0 %field_gradient.1 = (bf16[32,8,16,128]{3,2,1,0:T(8,128)(2,1)}, bf16[3,6,48,2048]{3,2,1,0:T(8,128)(2,1)}, bf16[32,8,16,128]{3,2,1,0:T(8,128)(2,1)}) custom-call(bf16[32,8,16,128]{3,2,1,0:T(8,128)(2,1)} %get-tuple-element.10.act_in, bf16[3,6,48,2048]{3,2,1,0:T(8,128)(2,1)} %get-tuple-element.11.wgrad_in, bf16[4,768,128]{2,1,0:T(8,128)(2,1)} %get-tuple-element.12.back_hbm, ...), custom_call_target="tpu_custom_call" | custom-call | tf_op jit(solution)/shard_map/field_gradient/pallas_call | solution.py:570

commit v4 on v2

--- a/solution.py
+++ b/solution.py
@@ -92,7 +92,7 @@
         table, field, cot, weight, pw, act, wgrad, zi, near, back_rows, zs, slope, spec, sums, prods, mix, t1, t1_last, t2,
         perm, perm_t, pw_fwd, pw_back, repeat, tile, group_sum,
         ws, wr, ns, nr,
-        ws_sem, wr_sem, ns_sem, nr_sem, load_sem, store_sem,
+        ws_sem, wr_sem, ns_sem, nr_sem, early_sem, load_sem, store_sem,
     ) = scratch
     w = lax.axis_index("wide")
     n = lax.axis_index("narrow")
@@ -110,8 +110,9 @@
         pltpu.make_async_copy(src, dst, load_sem.at[i])
         for i, (src, dst) in enumerate(
             (
-                (field_hbm, field),
+                (field_hbm.at[pl.ds(0, C // 2)], field.at[pl.ds(0, C // 2)]),
                 (table_hbm.at[z_part], table.at[z_part]),
+                (field_hbm.at[pl.ds(C // 2, C // 2)], field.at[pl.ds(C // 2, C // 2)]),
                 (pw_hbm, pw),
                 (table_hbm.at[other], table.at[other]),
                 (cot_hbm, cot),
@@ -141,8 +142,6 @@
 
     row = lax.broadcasted_iota(jnp.int32, (cells, cells), 0)
     col = lax.broadcasted_iota(jnp.int32, (cells, cells), 1)
-    perm[...] = ones_where(((row & 15) == (col >> 5)) & ((row >> 4) == (col & 31)))
-
     lane = lax.broadcasted_iota(jnp.int32, (1, 128), 1) >> 5
 
     def shift(value, groups):
@@ -155,22 +154,63 @@
             acc = jnp.where(lane == s, piece, acc)
         return acc
 
-    def depth(x, b, block):
+    def exchange(low, high, groups, first):
+        return (
+            jnp.where(first, low, shift(high, groups)),
+            jnp.where(first, shift(low, -groups), high),
+        )
+
+    def transpose_groups(p):
+        p0, p2 = exchange(p[0], p[2], 2, lane < 2)
+        p1, p3 = exchange(p[1], p[3], 2, lane < 2)
+        p0, p1 = exchange(p0, p1, 1, (lane & 1) == 0)
+        p2, p3 = exchange(p2, p3, 1, (lane & 1) == 0)
+        return [p0, p1, p2, p3]
+
+    def depth(x, hb, block):
         out = dot(z_fwd(), block, ((1,), (1,)))
-        zs[b, pl.ds(x, kk, stride=XL), :] = out
-
-    def send_wide(a, j):
+        for i in range(2):
+            zs[2 * hb + i, pl.ds(x, kk, stride=XL), :] = out[:, i * 128 : (i + 1) * 128]
+
+    def wide_copy(src, dst, to, send_sem, recv_sem):
+        pltpu.make_async_remote_copy(
+            src_ref=src,
+            dst_ref=dst,
+            send_sem=send_sem,
+            recv_sem=recv_sem,
+            device_id={"wide": to, "narrow": flip},
+            device_id_type=MESH,
+        ).start()
+
+    def send_wide(a, j, first=0, lanes=C * YL):
         @pl.loop(0, wide)
         def _(d):
             to = lax.rem(w + d, wide)
-            pltpu.make_async_remote_copy(
-                src_ref=ws.at[a, j, to],
-                dst_ref=wr.at[a, j, w],
-                send_sem=ws_sem.at[a, j],
-                recv_sem=wr_sem.at[a, j],
-                device_id={"wide": to, "narrow": flip},
-                device_id_type=MESH,
-            ).start()
+            window = (pl.ds(0, 2 * XL), pl.ds(first, lanes))
+            wide_copy(
+                ws.at[(a, j, to) + window], wr.at[(a, j, w) + window], to,
+                ws_sem.at[a, j], wr_sem.at[a, j],
+            )
+
+    early = (pl.ds(0, KL), pl.ds(0, wide), pl.ds(0, 2 * XL), pl.ds(0, 256))
+
+    def send_early(a):
+        @pl.loop(0, wide)
+        def _(d):
+            to = lax.rem(w + d, wide)
+            window = (pl.ds(0, 2 * XL), pl.ds(0, 256))
+            wide_copy(
+                ws.at[(a, pl.ds(0, KL), to) + window], wr.at[(a, pl.ds(0, KL), w) + window], to,
+                early_sem.at[0, a // 2], early_sem.at[1, a // 2],
+            )
+
+    def wait_early(buffer, a, which):
+        ref = buffer.at[(a,) + early]
+        pltpu.make_async_copy(ref, ref, early_sem.at[which, a // 2]).wait()
+
+    def wait_late(buffer, a, j, sem):
+        ref = buffer.at[a, j, pl.ds(0, wide), pl.ds(0, 2 * XL), pl.ds(256, 256)]
+        pltpu.make_async_copy(ref, ref, sem.at[a, j]).wait()
 
     def send_narrow(a, j, take, slot):
         nr[a, j, slot] = ns[a, j, take(n)]
@@ -194,30 +234,41 @@
     def part(j):
         return pl.ds(pl.multiple_of(j * rows_j, rows_j), rows_j)
 
-    def depth_out(a):
+    def pack(a, j, b):
+        block = zs[b, part(j), :].astype(BF16).reshape(wide, 2 * XL, 128)
+        ws[a, j, :, :, b * 128 : (b + 1) * 128] = block
+
+    def depth_out_early(a):
         @pl.loop(0, KL)
         def _(j):
-            block = jnp.concatenate([zs[b, part(j), :].astype(BF16) for b in range(4)], axis=1)
-            ws[a, j] = dot(block, perm[...]).astype(BF16).reshape(wide, 2 * XL, cells)
-            send_wide(a, j)
+            pack(a, j, 0)
+            pack(a, j, 1)
+
+        send_early(a)
+
+    def depth_out_late(a):
+        @pl.loop(0, KL)
+        def _(j):
+            pack(a, j, 2)
+            pack(a, j, 3)
+            send_wide(a, j, 256, 256)
 
     def x_forward(a, j):
-        wait_all(wr, a, j, wr_sem, wide)
+        wait_late(wr, a, j, wr_sem)
         out = dot(x_fwd(), wr[a, j].reshape(rows_j, cells))
-        for y in range(YL):
-            yb, g = y // 4, y % 4
+        out = dot(out.astype(BF16), perm[...])
+        for yb in range(4):
 
             def piece(kx, ri):
                 first = (kx * 2 + ri) * narrow
                 return out[first : first + narrow, yb * 128 : (yb + 1) * 128]
 
             for ri in range(2):
-                t1[pl.ds(ri * YL + y, narrow, stride=2 * YL), :] = pick(
-                    [shift(piece(s, ri), s - g) for s in range(4)]
-                )
-            t1_last[pl.ds(y, narrow, stride=YL), :] = pick(
-                [shift(piece(4 + s % 2, s // 2), s - g) for s in range(4)]
-            )
+                for g, value in enumerate(transpose_groups([piece(s, ri) for s in range(4)])):
+                    t1[pl.ds(ri * YL + 4 * yb + g, narrow, stride=2 * YL), :] = value
+            last = transpose_groups([piece(4 + s % 2, s // 2) for s in range(4)])
+            for g, value in enumerate(last):
+                t1_last[pl.ds(4 * yb + g, narrow, stride=YL), :] = value
         ns[a, j, :, : 2 * YL, :] = t1[...].astype(BF16).reshape(narrow, 2 * YL, 128)
         ns[a, j, :, 2 * YL :, :] = t1_last[...].astype(BF16).reshape(narrow, YL, 128)
         send_narrow(a, j, lambda to: to, flip)
@@ -313,19 +364,19 @@
                 [t1[pl.ds(ri * YL + y, narrow, stride=2 * YL), :] for y in ys] for ri in range(2)
             ]
             last = [t1_last[pl.ds(y, narrow, stride=YL), :] for y in ys]
-            for kx in range(KXL):
-                both = []
-                for ri in range(2):
-                    source = loaded[ri] if kx < 4 else last
-                    s = kx if kx < 4 else ri * 2 + kx - 4
-                    both.append(pick([shift(source[g], g - s) for g in range(4)]))
+            real, imag, last = [transpose_groups(p) for p in loaded + [last]]
+            pairs = list(zip(real, imag)) + [(last[0], last[2]), (last[1], last[3])]
+            for kx, pair in enumerate(pairs):
                 t2[kx * 2 * narrow : (kx + 1) * 2 * narrow, lanes] = jnp.concatenate(
-                    both, axis=0
+                    pair, axis=0
                 ).astype(BF16)
-        ws[a, j] = dot(x_inv(), t2[...]).astype(BF16).reshape(wide, 2 * XL, cells)
+        modes_cy = dot(t2[...], perm_t[...]).astype(BF16)
+        ws[a, j] = dot(x_inv(), modes_cy).astype(BF16).reshape(wide, 2 * XL, cells)
         send_wide(a, j)
 
     def through_modes(back):
+        wait_early(wr, 2 * back, 1)
+
         @pl.loop(0, KL + 2)
         def _(t):
             @pl.when(t < KL)
@@ -346,31 +397,34 @@
         @pl.loop(0, KL)
         def _(j):
             wait_all(wr, a, j, wr_sem, wide)
-            out = dot(wr[a, j].reshape(rows_j, cells), perm_t[...])
             for b in range(4):
-                block = out[:, b * 128 : (b + 1) * 128]
+                block = wr[a, j, :, :, b * 128 : (b + 1) * 128].reshape(rows_j, 128)
                 if a == 1:
-                    zi[b, part(j), :] = block
+                    zi[b, part(j), :] = block.astype(F32)
                 else:
-                    back_rows[b, part(j), :] = block.astype(BF16)
+                    back_rows[b, part(j), :] = block
 
     def pointwise(matrix, source):
-        @pl.loop(0, XL)
+        @pl.loop(0, XL // 2)
         def _(x):
-            near[x] = dot(matrix[...], source[:, x].reshape(cells, NZ))
-
-    loads[0].wait()
+            both = [source[:, 2 * x + i].reshape(cells, NZ) for i in range(2)]
+            out = dot(matrix[...], jnp.concatenate(both, axis=1))
+            for i in range(2):
+                near[2 * x + i] = out[:, i * NZ : (i + 1) * NZ]
+
     loads[1].wait()
-    for x in range(XL):
-        plane = field[:, x].reshape(cells, NZ)
-        for b in range(4):
-            depth(x, b, plane[b * 128 : (b + 1) * 128])
-
-    pl.semaphore_wait(barrier, wide + narrow - 1)
-    depth_out(0)
-
-    loads[2].wait()
+    for hb in range(2):
+        loads[2 * hb].wait()
+        for x in range(XL):
+            depth(x, hb, field[hb * 16 : (hb + 1) * 16, x].reshape(256, NZ))
+        if hb == 0:
+            pl.semaphore_wait(barrier, wide + narrow - 1)
+            depth_out_early(0)
+    depth_out_late(0)
+
     loads[3].wait()
+    loads[4].wait()
+    perm[...] = ones_where(((row & 15) == (col >> 5)) & ((row >> 4) == (col & 31)))
     perm_t[...] = ones_where(((row >> 5) == (col & 15)) & ((row & 31) == (col >> 4)))
     spread_row = lax.broadcasted_iota(jnp.int32, (cells, C), 0)
     spread_col = lax.broadcasted_iota(jnp.int32, (cells, C), 1)
@@ -390,32 +444,38 @@
     g_col = lax.broadcasted_iota(jnp.int32, (1024, 128), 1)
     group_sum[...] = ones_where((g_row >> 5) == (g_col & 31))
     pointwise(pw_fwd, field)
-    loads[4].wait()
     loads[5].wait()
+    loads[6].wait()
 
     through_modes(0)
     depth_in(1)
 
     root = 0.7978845608028654
 
-    @pl.loop(0, 4)
-    def _(b):
-        rows = pl.ds(pl.multiple_of(b * 128, 128), 128)
-        group = pl.ds(b * 8, 8)
+    @pl.loop(0, 2)
+    def _(hb):
+        rows = pl.ds(pl.multiple_of(hb * 256, 256), 256)
+        group = pl.ds(hb * 16, 16)
         for x in range(XL):
-            block = zi[b, pl.ds(x, kk, stride=XL), :].astype(BF16)
+            block = jnp.concatenate(
+                [zi[2 * hb + i, pl.ds(x, kk, stride=XL), :].astype(BF16) for i in range(2)], axis=1
+            )
             t = dot(block, z_fwd(), ((0,), (0,))) + near[x, rows, :]
             square = t * t
-            th = jnp.tanh(root * t * (1.0 + 0.044715 * square))
-            gate = 0.5 + 0.5 * th
-            act[group, x] = (t * gate).astype(BF16).reshape(8, YL, NZ)
-            grad = gate + (0.5 * root) * t * (1.0 - th * th) * (1.0 + 0.134145 * square)
-            up = cot[group, x].reshape(128, NZ).astype(F32)
+            gate = 0.5 + 0.5 * jnp.tanh(t * (root + (root * 0.044715) * square))
+            out = t * gate
+            act[group, x] = out.astype(BF16).reshape(16, YL, NZ)
+            grad = gate + out * (1.0 - gate) * (2.0 * root + (6.0 * root * 0.044715) * square)
+            up = cot[group, x].reshape(256, NZ).astype(F32)
             block = (up * grad).astype(BF16)
-            slope[group, x] = block.reshape(8, YL, NZ)
-            depth(x, b, block)
-
-    depth_out(2)
+            slope[group, x] = block.reshape(16, YL, NZ)
+            depth(x, hb, block)
+
+        @pl.when(hb == 0)
+        def _():
+            depth_out_early(2)
+
+    depth_out_late(2)
     stores = [
         pltpu.make_async_copy(src, dst, store_sem.at[i])
         for i, (src, dst) in enumerate(
@@ -435,8 +495,15 @@
     def _(a):
         @pl.loop(0, KL)
         def _(j):
-            wait_all(ws, a, j, ws_sem, wide)
             wait_all(ns, a, j, ns_sem, narrow - 1)
+
+    for a in (0, 2):
+        wait_early(ws, a, 0)
+
+        @pl.loop(0, KL)
+        def _(j):
+            wait_late(ws, a, j, ws_sem)
+            wait_all(ws, a + 1, j, ws_sem, wide)
 
     for store in stores:
         store.wait()
@@ -472,20 +539,25 @@
         )
         passed[-1][0].start()
     load_table.wait()
-    for b in range(4):
-        for load in loads[b]:
-            load.wait()
-        zi[b] = back[b].astype(F32)
+    for hb in range(2):
+        for b in (2 * hb, 2 * hb + 1):
+            for load in loads[b]:
+                load.wait()
+            zi[b] = back[b].astype(F32)
         for x in range(XL):
-            block = zi[b, pl.ds(x, kk, stride=XL), :].astype(BF16)
-            t = dot(block, table[...], ((0,), (0,))) + near[x, b * 128 : (b + 1) * 128, :]
-            fgrad[b * 8 : (b + 1) * 8, x] = t.astype(BF16).reshape(8, YL, NZ)
-        group = pl.ds(b * 8, 8)
-        stores.append(pltpu.make_async_copy(fgrad.at[group], fgrad_hbm.at[group], sem.at[17 + b]))
+            block = jnp.concatenate(
+                [zi[2 * hb + i, pl.ds(x, kk, stride=XL), :].astype(BF16) for i in range(2)], axis=1
+            )
+            rows = slice(hb * 256, (hb + 1) * 256)
+            t = dot(block, table[...], ((0,), (0,))) + near[x, rows, :]
+            fgrad[hb * 16 : (hb + 1) * 16, x] = t.astype(BF16).reshape(16, YL, NZ)
+        group = pl.ds(hb * 16, 16)
+        stores.append(pltpu.make_async_copy(fgrad.at[group], fgrad_hbm.at[group], sem.at[17 + hb]))
         stores[-1].start()
-        passed[b][0].wait()
-        passed[b][1].start()
-        stores.append(passed[b][1])
+        for i in (2 * hb, 2 * hb + 1):
+            passed[i][0].wait()
+            passed[i][1].start()
+            stores.append(passed[i][1])
     for store in stores:
         store.wait()
 
@@ -546,7 +618,8 @@
             pltpu.SemaphoreType.DMA((4, KL)),
             pltpu.SemaphoreType.DMA((4, KL)),
             pltpu.SemaphoreType.DMA((4, KL)),
-            pltpu.SemaphoreType.DMA((6,)),
+            pltpu.SemaphoreType.DMA((2, 2)),
+            pltpu.SemaphoreType.DMA((7,)),
             pltpu.SemaphoreType.DMA((4,)),
         ],
         compiler_params=pltpu.CompilerParams(

time: 85.1 us -> 86 us (1.011)
  Pallas kernels: 84.3 us -> 85.3 us
where the time goes in v4:
time: 86 us; the launch traced here: 85.9 us
  Pallas kernels  85.3 us (99%)
    pallas_call x1, Pallas kernels, on_device(): pl.pallas_call(functools.partial(kernel, wide, narrow, ky, total, places)...  80 us
    pallas_call x1, Pallas kernels, on_device(): pl.pallas_call(functools.partial(finish, kk), out_shape=(grid_like, weigh...  5.3 us

profile of v4, /device:TPU:1, one launch (start us, length us, event | category | flops | bytes accessed | tf_op | source)
XLA Modules:
  0.0 85.9 jit_solution(17302105320490588935)
XLA Ops:
  0.6 80.0 %spectral_layer.1 = (bf16[32,8,16,128]{3,2,1,0:T(8,128)(2,1)}, bf16[3,6,48,2048]{3,2,1,0:T(8,128)(2,1)}, bf16[4,768,128]{2,1,0:T(8,128)(2,1)}, f32[8,512,128]{2,1,0:T(8,128)}) custom-call(bf16[32,8,16,128]{3,2,1,0:T(8,128)(2,1)} %field_hbm.1, bf16[32,8,16,128]{3,2,1,0:T(8,128)(2,1)} %cot_hbm.1, bf16[3,6,48,2048]{3,2,1,0:T(8,128)(2,1)} %weight_hbm.1, ...), custom_call_target="tpu_custom_call" | custom-call | tf_op jit(solution)/shard_map/spectral_layer/pallas_call | solution.py:576
  80.6 5.3 %field_gradient.1 = (bf16[32,8,16,128]{3,2,1,0:T(8,128)(2,1)}, bf16[3,6,48,2048]{3,2,1,0:T(8,128)(2,1)}, bf16[32,8,16,128]{3,2,1,0:T(8,128)(2,1)}) custom-call(bf16[32,8,16,128]{3,2,1,0:T(8,128)(2,1)} %get-tuple-element.10.act_in, bf16[3,6,48,2048]{3,2,1,0:T(8,128)(2,1)} %get-tuple-element.11.wgrad_in, bf16[4,768,128]{2,1,0:T(8,128)(2,1)} %get-tuple-element.12.back_hbm, ...), custom_call_target="tpu_custom_call" | custom-call | tf_op jit(solution)/shard_map/field_gradient/pallas_call | solution.py:630

commit v5 on v4

--- a/solution.py
+++ b/solution.py
@@ -92,7 +92,7 @@
         table, field, cot, weight, pw, act, wgrad, zi, near, back_rows, zs, slope, spec, sums, prods, mix, t1, t1_last, t2,
         perm, perm_t, pw_fwd, pw_back, repeat, tile, group_sum,
         ws, wr, ns, nr,
-        ws_sem, wr_sem, ns_sem, nr_sem, early_sem, load_sem, store_sem,
+        ws_sem, wr_sem, ns_sem, nr_sem, load_sem, store_sem,
     ) = scratch
     w = lax.axis_index("wide")
     n = lax.axis_index("narrow")
@@ -172,90 +172,59 @@
         for i in range(2):
             zs[2 * hb + i, pl.ds(x, kk, stride=XL), :] = out[:, i * 128 : (i + 1) * 128]
 
-    def wide_copy(src, dst, to, send_sem, recv_sem):
-        pltpu.make_async_remote_copy(
-            src_ref=src,
-            dst_ref=dst,
-            send_sem=send_sem,
-            recv_sem=recv_sem,
-            device_id={"wide": to, "narrow": flip},
-            device_id_type=MESH,
-        ).start()
-
-    def send_wide(a, j, first=0, lanes=C * YL):
+    def send_wide(a, hb=None):
+        at = lambda ref, i: ref.at[a, i] if hb is None else ref.at[a, i, hb]
+
         @pl.loop(0, wide)
         def _(d):
             to = lax.rem(w + d, wide)
-            window = (pl.ds(0, 2 * XL), pl.ds(first, lanes))
-            wide_copy(
-                ws.at[(a, j, to) + window], wr.at[(a, j, w) + window], to,
-                ws_sem.at[a, j], wr_sem.at[a, j],
-            )
-
-    early = (pl.ds(0, KL), pl.ds(0, wide), pl.ds(0, 2 * XL), pl.ds(0, 256))
-
-    def send_early(a):
-        @pl.loop(0, wide)
-        def _(d):
-            to = lax.rem(w + d, wide)
-            window = (pl.ds(0, 2 * XL), pl.ds(0, 256))
-            wide_copy(
-                ws.at[(a, pl.ds(0, KL), to) + window], wr.at[(a, pl.ds(0, KL), w) + window], to,
-                early_sem.at[0, a // 2], early_sem.at[1, a // 2],
-            )
-
-    def wait_early(buffer, a, which):
-        ref = buffer.at[(a,) + early]
-        pltpu.make_async_copy(ref, ref, early_sem.at[which, a // 2]).wait()
-
-    def wait_late(buffer, a, j, sem):
-        ref = buffer.at[a, j, pl.ds(0, wide), pl.ds(0, 2 * XL), pl.ds(256, 256)]
-        pltpu.make_async_copy(ref, ref, sem.at[a, j]).wait()
-
-    def send_narrow(a, j, take, slot):
-        nr[a, j, slot] = ns[a, j, take(n)]
+            pltpu.make_async_remote_copy(
+                src_ref=at(ws, to),
+                dst_ref=at(wr, w),
+                send_sem=ws_sem.at[a, hb or 0],
+                recv_sem=wr_sem.at[a, hb or 0],
+                device_id={"wide": to, "narrow": flip},
+                device_id_type=MESH,
+            ).start()
+
+    def wait_wide(buffer, sem, a, hb=None):
+        ref = buffer.at[a] if hb is None else buffer.at[a, pl.ds(0, wide), hb]
+        pltpu.make_async_copy(ref, ref, sem.at[a, hb or 0]).wait()
+
+    def send_narrow(a, take, slot):
+        nr[a, slot] = ns[a, take(n)]
 
         @pl.loop(1, narrow)
         def _(d):
             to = lax.rem(n + d, narrow)
             pltpu.make_async_remote_copy(
-                src_ref=ns.at[a, j, take(to)],
-                dst_ref=nr.at[a, j, slot],
-                send_sem=ns_sem.at[a, j],
-                recv_sem=nr_sem.at[a, j],
+                src_ref=ns.at[a, take(to)],
+                dst_ref=nr.at[a, slot],
+                send_sem=ns_sem.at[a],
+                recv_sem=nr_sem.at[a],
                 device_id={"narrow": to},
                 device_id_type=MESH,
             ).start()
 
-    def wait_all(buffer, a, j, sem, count):
-        ref = buffer.at[a, j, pl.ds(0, count)]
-        pltpu.make_async_copy(ref, ref, sem.at[a, j]).wait()
+    def wait_narrow(buffer, sem, a):
+        ref = buffer.at[a, pl.ds(0, narrow - 1)]
+        pltpu.make_async_copy(ref, ref, sem.at[a]).wait()
 
     def part(j):
         return pl.ds(pl.multiple_of(j * rows_j, rows_j), rows_j)
 
-    def pack(a, j, b):
-        block = zs[b, part(j), :].astype(BF16).reshape(wide, 2 * XL, 128)
-        ws[a, j, :, :, b * 128 : (b + 1) * 128] = block
-
-    def depth_out_early(a):
+    def depth_out(a, hb):
         @pl.loop(0, KL)
         def _(j):
-            pack(a, j, 0)
-            pack(a, j, 1)
-
-        send_early(a)
-
-    def depth_out_late(a):
-        @pl.loop(0, KL)
-        def _(j):
-            pack(a, j, 2)
-            pack(a, j, 3)
-            send_wide(a, j, 256, 256)
+            for i in range(2):
+                block = zs[2 * hb + i, part(j), :].astype(BF16).reshape(wide, 2 * XL, 128)
+                ws[a, :, hb, j, :, i * 128 : (i + 1) * 128] = block
+
+        send_wide(a, hb)
 
     def x_forward(a, j):
-        wait_late(wr, a, j, wr_sem)
-        out = dot(x_fwd(), wr[a, j].reshape(rows_j, cells))
+        block = [wr[a, :, hb, j].reshape(rows_j, 256) for hb in range(2)]
+        out = dot(x_fwd(), jnp.concatenate(block, axis=1))
         out = dot(out.astype(BF16), perm[...])
         for yb in range(4):
 
@@ -269,14 +238,12 @@
             last = transpose_groups([piece(4 + s % 2, s // 2) for s in range(4)])
             for g, value in enumerate(last):
                 t1_last[pl.ds(4 * yb + g, narrow, stride=YL), :] = value
-        ns[a, j, :, : 2 * YL, :] = t1[...].astype(BF16).reshape(narrow, 2 * YL, 128)
-        ns[a, j, :, 2 * YL :, :] = t1_last[...].astype(BF16).reshape(narrow, YL, 128)
-        send_narrow(a, j, lambda to: to, flip)
+        ns[a, :, j, : 2 * YL, :] = t1[...].astype(BF16).reshape(narrow, 2 * YL, 128)
+        ns[a, :, j, 2 * YL :, :] = t1_last[...].astype(BF16).reshape(narrow, YL, 128)
 
     def y_forward(a, j, which):
-        wait_all(nr, a, j, nr_sem, narrow - 1)
-        first = dot(y_fwd(), nr[a, j, :, : 2 * YL, :].reshape(narrow * 2 * YL, 128))
-        both = dot(y_fwd_split(), nr[a, j, :, 2 * YL :, :].reshape(narrow * YL, 128))
+        first = dot(y_fwd(), nr[a, :, j, : 2 * YL, :].reshape(narrow * 2 * YL, 128))
+        both = dot(y_fwd_split(), nr[a, :, j, 2 * YL :, :].reshape(narrow * YL, 128))
         last = both[: 2 * ky] + shift(both[2 * ky :], 2)
         for kx in range(KXL):
             source = first if kx < 4 else last
@@ -346,17 +313,15 @@
 
     def y_inverse(a, j):
         first = dot(y_inv(), mix[0]).astype(BF16)
-        ns[a, j, :, : 2 * YL, :] = first.reshape(narrow, 2 * YL, 128)
+        ns[a, :, j, : 2 * YL, :] = first.reshape(narrow, 2 * YL, 128)
         both = dot(y_inv_split(), mix[1])
         split = narrow * YL
         last = jnp.where(lane < 2, both[:split], shift(both[split:], 2)).astype(BF16)
-        ns[a, j, :, 2 * YL :, :] = last.reshape(narrow, YL, 128)
-        send_narrow(a, j, lambda to: lax.rem(to + half, narrow), n)
+        ns[a, :, j, 2 * YL :, :] = last.reshape(narrow, YL, 128)
 
     def x_inverse(a, j):
-        wait_all(nr, a, j, nr_sem, narrow - 1)
-        t1[...] = nr[a, j, :, : 2 * YL, :].reshape(narrow * 2 * YL, 128).astype(F32)
-        t1_last[...] = nr[a, j, :, 2 * YL :, :].reshape(narrow * YL, 128).astype(F32)
+        t1[...] = nr[a, :, j, : 2 * YL, :].reshape(narrow * 2 * YL, 128).astype(F32)
+        t1_last[...] = nr[a, :, j, 2 * YL :, :].reshape(narrow * YL, 128).astype(F32)
         for yb in range(4):
             lanes = slice(yb * 128, (yb + 1) * 128)
             ys = [4 * yb + g for g in range(4)]
@@ -371,34 +336,46 @@
                     pair, axis=0
                 ).astype(BF16)
         modes_cy = dot(t2[...], perm_t[...]).astype(BF16)
-        ws[a, j] = dot(x_inv(), modes_cy).astype(BF16).reshape(wide, 2 * XL, cells)
-        send_wide(a, j)
-
-    def through_modes(back):
-        wait_early(wr, 2 * back, 1)
-
-        @pl.loop(0, KL + 2)
-        def _(t):
-            @pl.when(t < KL)
-            def _():
-                x_forward(2 * back, t)
-
-            @pl.when((t >= 1) & (t <= KL))
-            def _():
-                y_forward(2 * back, t - 1, back)
-                mix_back(t - 1) if back else mix_forward(t - 1)
-                y_inverse(2 * back + 1, t - 1)
-
-            @pl.when(t >= 2)
-            def _():
-                x_inverse(2 * back + 1, t - 2)
-
-    def depth_in(a):
+        out = dot(x_inv(), modes_cy).astype(BF16)
+        for hb in range(2):
+            ws[a, :, hb, j] = out[:, hb * 256 : (hb + 1) * 256].reshape(wide, 2 * XL, 256)
+
+    def each(step):
         @pl.loop(0, KL)
         def _(j):
-            wait_all(wr, a, j, wr_sem, wide)
+            step(j)
+
+    def through_modes(back):
+        first, second = 2 * back, 2 * back + 1
+
+        def mode_step(j):
+            y_forward(first, j, back)
+            mix_back(j) if back else mix_forward(j)
+            y_inverse(second, j)
+
+        for hb in range(2):
+            wait_wide(wr, wr_sem, first, hb)
+        each(lambda j: x_forward(first, j))
+        send_narrow(first, lambda to: to, flip)
+        wait_narrow(nr, nr_sem, first)
+        each(mode_step)
+        send_narrow(second, lambda to: lax.rem(to + half, narrow), n)
+        if back:
+            weight_gradient(0)
+        wait_narrow(nr, nr_sem, second)
+        each(lambda j: x_inverse(second, j))
+        send_wide(second)
+        if back:
+            pl.loop(1, KL)(weight_gradient)
+
+    def depth_in(a):
+        wait_wide(wr, wr_sem, a)
+
+        @pl.loop(0, KL)
+        def _(j):
             for b in range(4):
-                block = wr[a, j, :, :, b * 128 : (b + 1) * 128].reshape(rows_j, 128)
+                hb, i = b // 2, b % 2
+                block = wr[a, :, hb, j, :, i * 128 : (i + 1) * 128].reshape(rows_j, 128)
                 if a == 1:
                     zi[b, part(j), :] = block.astype(F32)
                 else:
@@ -419,8 +396,7 @@
             depth(x, hb, field[hb * 16 : (hb + 1) * 16, x].reshape(256, NZ))
         if hb == 0:
             pl.semaphore_wait(barrier, wide + narrow - 1)
-            depth_out_early(0)
-    depth_out_late(0)
+        depth_out(0, hb)
 
     loads[3].wait()
     loads[4].wait()
@@ -471,11 +447,12 @@
             slope[group, x] = block.reshape(16, YL, NZ)
             depth(x, hb, block)
 
-        @pl.when(hb == 0)
-        def _():
-            depth_out_early(2)
-
-    depth_out_late(2)
+        for i in range(2):
+
+            @pl.when(hb == i)
+            def _():
+                depth_out(2, i)
+
     stores = [
         pltpu.make_async_copy(src, dst, store_sem.at[i])
         for i, (src, dst) in enumerate(
@@ -486,24 +463,14 @@
     pointwise(pw_back, slope)
     stores[1].start()
     through_modes(1)
-    pl.loop(0, KL)(weight_gradient)
     stores[2].start()
     depth_in(3)
     stores[3].start()
 
-    @pl.loop(0, 4)
-    def _(a):
-        @pl.loop(0, KL)
-        def _(j):
-            wait_all(ns, a, j, ns_sem, narrow - 1)
-
-    for a in (0, 2):
-        wait_early(ws, a, 0)
-
-        @pl.loop(0, KL)
-        def _(j):
-            wait_late(ws, a, j, ws_sem)
-            wait_all(ws, a + 1, j, ws_sem, wide)
+    for a in range(4):
+        wait_narrow(ns, ns_sem, a)
+        for hb in (0, 1) if a % 2 == 0 else (None,):
+            wait_wide(ws, ws_sem, a, hb)
 
     for store in stores:
         store.wait()
@@ -610,15 +577,14 @@
             pltpu.VMEM((128, 1024), BF16),
             pltpu.VMEM((128, 128), BF16),
             pltpu.VMEM((1024, 128), BF16),
-            pltpu.VMEM((4, KL, wide, 2 * XL, cells), BF16),
-            pltpu.VMEM((4, KL, wide, 2 * XL, cells), BF16),
-            pltpu.VMEM((4, KL, narrow, 3 * YL, 128), BF16),
-            pltpu.VMEM((4, KL, narrow, 3 * YL, 128), BF16),
-            pltpu.SemaphoreType.DMA((4, KL)),
-            pltpu.SemaphoreType.DMA((4, KL)),
-            pltpu.SemaphoreType.DMA((4, KL)),
-            pltpu.SemaphoreType.DMA((4, KL)),
-            pltpu.SemaphoreType.DMA((2, 2)),
+            pltpu.VMEM((4, wide, 2, KL, 2 * XL, 256), BF16),
+            pltpu.VMEM((4, wide, 2, KL, 2 * XL, 256), BF16),
+            pltpu.VMEM((4, narrow, KL, 3 * YL, 128), BF16),
+            pltpu.VMEM((4, narrow, KL, 3 * YL, 128), BF16),
+            pltpu.SemaphoreType.DMA((4, 2)),
+            pltpu.SemaphoreType.DMA((4, 2)),
+            pltpu.SemaphoreType.DMA((4,)),
+            pltpu.SemaphoreType.DMA((4,)),
             pltpu.SemaphoreType.DMA((7,)),
             pltpu.SemaphoreType.DMA((4,)),
         ],

time: 86 us -> 98.7 us (1.15)
  Pallas kernels: 85.3 us -> 97.9 us
    pallas_call x1, Pallas kernels: 80 us -> 92.6 us  [on_device(): pl.pallas_call(functools.partial(kernel, wide, narrow, ky, total, places)...]
where the time goes in v5:
time: 98.7 us; the launch traced here: 98.6 us
  Pallas kernels  97.9 us (99%)
    pallas_call x1, Pallas kernels, on_device(): pl.pallas_call(functools.partial(kernel, wide, narrow, ky, total, places)...  92.6 us
    pallas_call x1, Pallas kernels, on_device(): pl.pallas_call(functools.partial(finish, kk), out_shape=(grid_like, weigh...  5.3 us

profile of v5, /device:TPU:1, one launch (start us, length us, event | category | flops | bytes accessed | tf_op | source)
XLA Modules:
  0.0 98.6 jit_solution(12975456468305672546)
XLA Ops:
  0.6 92.6 %spectral_layer.1 = (bf16[32,8,16,128]{3,2,1,0:T(8,128)(2,1)}, bf16[3,6,48,2048]{3,2,1,0:T(8,128)(2,1)}, bf16[4,768,128]{2,1,0:T(8,128)(2,1)}, f32[8,512,128]{2,1,0:T(8,128)}) custom-call(bf16[32,8,16,128]{3,2,1,0:T(8,128)(2,1)} %field_hbm.1, bf16[32,8,16,128]{3,2,1,0:T(8,128)(2,1)} %cot_hbm.1, bf16[3,6,48,2048]{3,2,1,0:T(8,128)(2,1)} %weight_hbm.1, ...), custom_call_target="tpu_custom_call" | custom-call | tf_op jit(solution)/shard_map/spectral_layer/pallas_call | solution.py:543
  93.3 5.3 %field_gradient.1 = (bf16[32,8,16,128]{3,2,1,0:T(8,128)(2,1)}, bf16[3,6,48,2048]{3,2,1,0:T(8,128)(2,1)}, bf16[32,8,16,128]{3,2,1,0:T(8,128)(2,1)}) custom-call(bf16[32,8,16,128]{3,2,1,0:T(8,128)(2,1)} %get-tuple-element.10.act_in, bf16[3,6,48,2048]{3,2,1,0:T(8,128)(2,1)} %get-tuple-element.11.wgrad_in, bf16[4,768,128]{2,1,0:T(8,128)(2,1)} %get-tuple-element.12.back_hbm, ...), custom_call_target="tpu_custom_call" | custom-call | tf_op jit(solution)/shard_map/field_gradient/pallas_call | solution.py:596

commit v6 on v5

--- a/solution.py
+++ b/solution.py
@@ -89,10 +89,10 @@
     *scratch,
 ):
     (
-        table, field, cot, weight, pw, act, wgrad, zi, near, back_rows, zs, slope, spec, sums, prods, mix, t1, t1_last, t2,
+        table, field, cot, weight, pw, act, wgrad, zi, near, zs, slope, spec, sums, prods, mix, t1, t1_last, t2,
         perm, perm_t, pw_fwd, pw_back, repeat, tile, group_sum,
-        ws, wr, ns, nr,
-        ws_sem, wr_sem, ns_sem, nr_sem, load_sem, store_sem,
+        fs, fr, ls, lr, ns, nr,
+        fs_sem, fr_sem, ls_sem, lr_sem, ns_sem, nr_sem, load_sem, store_sem,
     ) = scratch
     w = lax.axis_index("wide")
     n = lax.axis_index("narrow")
@@ -172,43 +172,59 @@
         for i in range(2):
             zs[2 * hb + i, pl.ds(x, kk, stride=XL), :] = out[:, i * 128 : (i + 1) * 128]
 
-    def send_wide(a, hb=None):
-        at = lambda ref, i: ref.at[a, i] if hb is None else ref.at[a, i, hb]
-
+    def send_wide(src, dst, send_sem, recv_sem):
         @pl.loop(0, wide)
         def _(d):
             to = lax.rem(w + d, wide)
             pltpu.make_async_remote_copy(
-                src_ref=at(ws, to),
-                dst_ref=at(wr, w),
-                send_sem=ws_sem.at[a, hb or 0],
-                recv_sem=wr_sem.at[a, hb or 0],
+                src_ref=src(to),
+                dst_ref=dst(w),
+                send_sem=send_sem,
+                recv_sem=recv_sem,
                 device_id={"wide": to, "narrow": flip},
                 device_id_type=MESH,
             ).start()
 
-    def wait_wide(buffer, sem, a, hb=None):
-        ref = buffer.at[a] if hb is None else buffer.at[a, pl.ds(0, wide), hb]
-        pltpu.make_async_copy(ref, ref, sem.at[a, hb or 0]).wait()
-
-    def send_narrow(a, take, slot):
-        nr[a, slot] = ns[a, take(n)]
+    def wait(ref, sem):
+        pltpu.make_async_copy(ref, ref, sem).wait()
+
+    def send_first(a, hb):
+        send_wide(
+            lambda to: fs.at[a, to, hb], lambda me: fr.at[a, me, hb],
+            fs_sem.at[a, hb], fr_sem.at[a, hb],
+        )
+
+    def wait_first(buffer, sem, a, hb):
+        wait(buffer.at[a, pl.ds(0, wide), hb], sem.at[a, hb])
+
+    chunks = (pl.ds(0, KL - 1), pl.ds(KL - 1, 1))
+
+    def send_last(a, c):
+        send_wide(
+            lambda to: ls.at[a, to, chunks[c]], lambda me: lr.at[a, me, chunks[c]],
+            ls_sem.at[a, c], lr_sem.at[a, c],
+        )
+
+    def wait_last(buffer, sem, a, c):
+        wait(buffer.at[a, pl.ds(0, wide), chunks[c]], sem.at[a, c])
+
+    def send_narrow(a, i, j, take, slot):
+        nr[a, i, j, slot] = ns[a, i, j, take(n)]
 
         @pl.loop(1, narrow)
         def _(d):
             to = lax.rem(n + d, narrow)
             pltpu.make_async_remote_copy(
-                src_ref=ns.at[a, take(to)],
-                dst_ref=nr.at[a, slot],
-                send_sem=ns_sem.at[a],
-                recv_sem=nr_sem.at[a],
+                src_ref=ns.at[a, i, j, take(to)],
+                dst_ref=nr.at[a, i, j, slot],
+                send_sem=ns_sem.at[a, i, j],
+                recv_sem=nr_sem.at[a, i, j],
                 device_id={"narrow": to},
                 device_id_type=MESH,
             ).start()
 
-    def wait_narrow(buffer, sem, a):
-        ref = buffer.at[a, pl.ds(0, narrow - 1)]
-        pltpu.make_async_copy(ref, ref, sem.at[a]).wait()
+    def wait_narrow(buffer, sem, a, i, j):
+        wait(buffer.at[a, i, j, pl.ds(0, narrow - 1)], sem.at[a, i, j])
 
     def part(j):
         return pl.ds(pl.multiple_of(j * rows_j, rows_j), rows_j)
@@ -218,12 +234,12 @@
         def _(j):
             for i in range(2):
                 block = zs[2 * hb + i, part(j), :].astype(BF16).reshape(wide, 2 * XL, 128)
-                ws[a, :, hb, j, :, i * 128 : (i + 1) * 128] = block
-
-        send_wide(a, hb)
+                fs[a, :, hb, j, :, i * 128 : (i + 1) * 128] = block
+
+        send_first(a, hb)
 
     def x_forward(a, j):
-        block = [wr[a, :, hb, j].reshape(rows_j, 256) for hb in range(2)]
+        block = [fr[a, :, hb, j].reshape(rows_j, 256) for hb in range(2)]
         out = dot(x_fwd(), jnp.concatenate(block, axis=1))
         out = dot(out.astype(BF16), perm[...])
         for yb in range(4):
@@ -238,16 +254,18 @@
             last = transpose_groups([piece(4 + s % 2, s // 2) for s in range(4)])
             for g, value in enumerate(last):
                 t1_last[pl.ds(4 * yb + g, narrow, stride=YL), :] = value
-        ns[a, :, j, : 2 * YL, :] = t1[...].astype(BF16).reshape(narrow, 2 * YL, 128)
-        ns[a, :, j, 2 * YL :, :] = t1_last[...].astype(BF16).reshape(narrow, YL, 128)
-
-    def y_forward(a, j, which):
-        first = dot(y_fwd(), nr[a, :, j, : 2 * YL, :].reshape(narrow * 2 * YL, 128))
-        both = dot(y_fwd_split(), nr[a, :, j, 2 * YL :, :].reshape(narrow * YL, 128))
+        ns[a, 0, j, :, : 2 * YL, :] = t1[...].astype(BF16).reshape(narrow, 2 * YL, 128)
+        ns[a, 0, j, :, 2 * YL :, :] = t1_last[...].astype(BF16).reshape(narrow, YL, 128)
+        send_narrow(a, 0, j, lambda to: to, flip)
+
+    def y_forward(a, j):
+        wait_narrow(nr, nr_sem, a, 0, j)
+        first = dot(y_fwd(), nr[a, 0, j, :, : 2 * YL, :].reshape(narrow * 2 * YL, 128))
+        both = dot(y_fwd_split(), nr[a, 0, j, :, 2 * YL :, :].reshape(narrow * YL, 128))
         last = both[: 2 * ky] + shift(both[2 * ky :], 2)
         for kx in range(KXL):
             source = first if kx < 4 else last
-            spec[which, j, kx * 2 * ky : (kx + 1) * 2 * ky, :] = shift(source, -(kx % 4)).astype(BF16)
+            spec[a, j, kx * 2 * ky : (kx + 1) * 2 * ky, :] = shift(source, -(kx % 4)).astype(BF16)
 
     def scale(j):
         return jnp.where(w * KL + j == 0, 1.0, 2.0).astype(F32) / total
@@ -313,15 +331,17 @@
 
     def y_inverse(a, j):
         first = dot(y_inv(), mix[0]).astype(BF16)
-        ns[a, :, j, : 2 * YL, :] = first.reshape(narrow, 2 * YL, 128)
+        ns[a, 1, j, :, : 2 * YL, :] = first.reshape(narrow, 2 * YL, 128)
         both = dot(y_inv_split(), mix[1])
         split = narrow * YL
         last = jnp.where(lane < 2, both[:split], shift(both[split:], 2)).astype(BF16)
-        ns[a, :, j, 2 * YL :, :] = last.reshape(narrow, YL, 128)
+        ns[a, 1, j, :, 2 * YL :, :] = last.reshape(narrow, YL, 128)
+        send_narrow(a, 1, j, lambda to: lax.rem(to + half, narrow), n)
 
     def x_inverse(a, j):
-        t1[...] = nr[a, :, j, : 2 * YL, :].reshape(narrow * 2 * YL, 128).astype(F32)
-        t1_last[...] = nr[a, :, j, 2 * YL :, :].reshape(narrow * YL, 128).astype(F32)
+        wait_narrow(nr, nr_sem, a, 1, j)
+        t1[...] = nr[a, 1, j, :, : 2 * YL, :].reshape(narrow * 2 * YL, 128).astype(F32)
+        t1_last[...] = nr[a, 1, j, :, 2 * YL :, :].reshape(narrow * YL, 128).astype(F32)
         for yb in range(4):
             lanes = slice(yb * 128, (yb + 1) * 128)
             ys = [4 * yb + g for g in range(4)]
@@ -337,49 +357,52 @@
                 ).astype(BF16)
         modes_cy = dot(t2[...], perm_t[...]).astype(BF16)
         out = dot(x_inv(), modes_cy).astype(BF16)
-        for hb in range(2):
-            ws[a, :, hb, j] = out[:, hb * 256 : (hb + 1) * 256].reshape(wide, 2 * XL, 256)
+        ls[a, :, j] = out.reshape(wide, 2 * XL, cells)
 
     def each(step):
         @pl.loop(0, KL)
         def _(j):
             step(j)
 
-    def through_modes(back):
-        first, second = 2 * back, 2 * back + 1
-
+    def through_modes(a):
         def mode_step(j):
-            y_forward(first, j, back)
-            mix_back(j) if back else mix_forward(j)
-            y_inverse(second, j)
+            y_forward(a, j)
+            mix_back(j) if a else mix_forward(j)
+            y_inverse(a, j)
 
         for hb in range(2):
-            wait_wide(wr, wr_sem, first, hb)
-        each(lambda j: x_forward(first, j))
-        send_narrow(first, lambda to: to, flip)
-        wait_narrow(nr, nr_sem, first)
+            wait_first(fr, fr_sem, a, hb)
+        each(lambda j: x_forward(a, j))
         each(mode_step)
-        send_narrow(second, lambda to: lax.rem(to + half, narrow), n)
-        if back:
-            weight_gradient(0)
-        wait_narrow(nr, nr_sem, second)
-        each(lambda j: x_inverse(second, j))
-        send_wide(second)
-        if back:
-            pl.loop(1, KL)(weight_gradient)
-
-    def depth_in(a):
-        wait_wide(wr, wr_sem, a)
 
         @pl.loop(0, KL)
         def _(j):
-            for b in range(4):
-                hb, i = b // 2, b % 2
-                block = wr[a, :, hb, j, :, i * 128 : (i + 1) * 128].reshape(rows_j, 128)
-                if a == 1:
-                    zi[b, part(j), :] = block.astype(F32)
-                else:
-                    back_rows[b, part(j), :] = block
+            if a:
+
+                @pl.when(j == KL - 1)
+                def _():
+                    weight_gradient(0)
+
+            x_inverse(a, j)
+
+            for c, j_last in enumerate((KL - 2, KL - 1)):
+
+                @pl.when(j == j_last)
+                def _():
+                    send_last(a, c)
+
+        if a:
+            pl.loop(1, KL)(weight_gradient)
+
+    def depth_in():
+        for c in range(2):
+            wait_last(lr, lr_sem, 0, c)
+        for b in range(4):
+
+            @pl.loop(0, KL)
+            def _(j):
+                block = lr[0, :, j, :, b * 128 : (b + 1) * 128].reshape(rows_j, 128)
+                zi[b, part(j), :] = block.astype(F32)
 
     def pointwise(matrix, source):
         @pl.loop(0, XL // 2)
@@ -424,7 +447,7 @@
     loads[6].wait()
 
     through_modes(0)
-    depth_in(1)
+    depth_in()
 
     root = 0.7978845608028654
 
@@ -451,12 +474,18 @@
 
             @pl.when(hb == i)
             def _():
-                depth_out(2, i)
+                depth_out(1, i)
 
     stores = [
         pltpu.make_async_copy(src, dst, store_sem.at[i])
         for i, (src, dst) in enumerate(
-            ((act, act_hbm), (near, near_hbm), (wgrad, wgrad_hbm), (back_rows, back_hbm))
+            (
+                (act, act_hbm),
+                (near, near_hbm),
+                (wgrad, wgrad_hbm),
+                (lr.at[1, :, chunks[0]], back_hbm.at[:, chunks[0]]),
+                (lr.at[1, :, chunks[1]], back_hbm.at[:, chunks[1]]),
+            )
         )
     ]
     stores[0].start()
@@ -464,13 +493,16 @@
     stores[1].start()
     through_modes(1)
     stores[2].start()
-    depth_in(3)
-    stores[3].start()
-
-    for a in range(4):
-        wait_narrow(ns, ns_sem, a)
-        for hb in (0, 1) if a % 2 == 0 else (None,):
-            wait_wide(ws, ws_sem, a, hb)
+    for c in range(2):
+        wait_last(lr, lr_sem, 1, c)
+        stores[3 + c].start()
+
+    for a in range(2):
+        for i in range(2):
+            wait_first(fs, fs_sem, a, i)
+            wait_last(ls, ls_sem, a, i)
+            for j in range(KL):
+                wait_narrow(ns, ns_sem, a, i, j)
 
     for store in stores:
         store.wait()
@@ -484,12 +516,14 @@
     load_table = pltpu.make_async_copy(table_hbm.at[pl.ds(0, kk)], table, sem.at[0])
     load_table.start()
     loads, passed, stores = [], [], []
-    for b in range(4):
-        rows = pl.ds(b * 128, 128)
+    for hb in range(2):
+        part = pl.ds(hb * 256, 256)
         loads.append(
             (
-                pltpu.make_async_copy(back_hbm.at[b], back.at[b], sem.at[1 + b]),
-                pltpu.make_async_copy(near_hbm.at[:, rows], near.at[:, rows], sem.at[5 + b]),
+                pltpu.make_async_copy(
+                    back_hbm.at[:, :, :, part], back.at[:, :, :, part], sem.at[1 + hb]
+                ),
+                pltpu.make_async_copy(near_hbm.at[:, part], near.at[:, part], sem.at[5 + hb]),
             )
         )
         for load in loads[-1]:
@@ -507,10 +541,13 @@
         passed[-1][0].start()
     load_table.wait()
     for hb in range(2):
+        for load in loads[hb]:
+            load.wait()
         for b in (2 * hb, 2 * hb + 1):
-            for load in loads[b]:
-                load.wait()
-            zi[b] = back[b].astype(F32)
+            for j in range(KL):
+                rows = back.shape[0] * 2 * XL
+                block = back[:, j, :, b * 128 : (b + 1) * 128].reshape(rows, 128)
+                zi[b, j * rows : (j + 1) * rows, :] = block.astype(F32)
         for x in range(XL):
             block = jnp.concatenate(
                 [zi[2 * hb + i, pl.ds(x, kk, stride=XL), :].astype(BF16) for i in range(2)], axis=1
@@ -545,7 +582,7 @@
         out_shape=(
             grid_like,
             weight_like,
-            jax.ShapeDtypeStruct((4, kk * XL, 128), BF16),
+            jax.ShapeDtypeStruct((wide, KL, 2 * XL, cells), BF16),
             jax.ShapeDtypeStruct((XL, cells, NZ), F32),
         ),
         in_specs=[hbm] * 5,
@@ -560,7 +597,6 @@
             pltpu.VMEM(weight.shape, BF16),
             pltpu.VMEM((4, kk * XL, 128), F32),
             pltpu.VMEM((XL, cells, NZ), F32),
-            pltpu.VMEM((4, kk * XL, 128), BF16),
             pltpu.VMEM((4, kk * XL, 128), F32),
             pltpu.VMEM(field.shape, BF16),
             pltpu.VMEM((2, KL, modes, 128), BF16),
@@ -577,16 +613,20 @@
             pltpu.VMEM((128, 1024), BF16),
             pltpu.VMEM((128, 128), BF16),
             pltpu.VMEM((1024, 128), BF16),
-            pltpu.VMEM((4, wide, 2, KL, 2 * XL, 256), BF16),
-            pltpu.VMEM((4, wide, 2, KL, 2 * XL, 256), BF16),
-            pltpu.VMEM((4, narrow, KL, 3 * YL, 128), BF16),
-            pltpu.VMEM((4, narrow, KL, 3 * YL, 128), BF16),
-            pltpu.SemaphoreType.DMA((4, 2)),
-            pltpu.SemaphoreType.DMA((4, 2)),
-            pltpu.SemaphoreType.DMA((4,)),
-            pltpu.SemaphoreType.DMA((4,)),
+            pltpu.VMEM((2, wide, 2, KL, 2 * XL, 256), BF16),
+            pltpu.VMEM((2, wide, 2, KL, 2 * XL, 256), BF16),
+            pltpu.VMEM((2, wide, KL, 2 * XL, cells), BF16),
+            pltpu.VMEM((2, wide, KL, 2 * XL, cells), BF16),
+            pltpu.VMEM((2, 2, KL, narrow, 3 * YL, 128), BF16),
+            pltpu.VMEM((2, 2, KL, narrow, 3 * YL, 128), BF16),
+            pltpu.SemaphoreType.DMA((2, 2)),
+            pltpu.SemaphoreType.DMA((2, 2)),
+            pltpu.SemaphoreType.DMA((2, 2)),
+            pltpu.SemaphoreType.DMA((2, 2)),
+            pltpu.SemaphoreType.DMA((2, 2, KL)),
+            pltpu.SemaphoreType.DMA((2, 2, KL)),
             pltpu.SemaphoreType.DMA((7,)),
-            pltpu.SemaphoreType.DMA((4,)),
+            pltpu.SemaphoreType.DMA((5,)),
         ],
         compiler_params=pltpu.CompilerParams(
             collective_id=0, has_side_effects=True, vmem_limit_bytes=VMEM_BYTES
@@ -599,7 +639,7 @@
         in_specs=[hbm] * 5,
         out_specs=(hbm,) * 3,
         scratch_shapes=[
-            pltpu.VMEM((4, kk * XL, 128), BF16),
+            pltpu.VMEM((wide, KL, 2 * XL, cells), BF16),
             pltpu.VMEM((XL, cells, NZ), F32),
             pltpu.VMEM((kk, NZ), BF16),
             pltpu.VMEM((4, kk * XL, 128), F32),

time: 98.7 us -> 85.4 us (0.87)
  Pallas kernels: 97.9 us -> 84.6 us
    pallas_call x1, Pallas kernels: 92.6 us -> 79.4 us  [on_device(): pl.pallas_call(functools.partial(kernel, wide, narrow, ky, total, places)...]
where the time goes in v6:
time: 85.4 us; the launch traced here: 85.3 us
  Pallas kernels  84.6 us (99%)
    pallas_call x1, Pallas kernels, on_device(): pl.pallas_call(functools.partial(kernel, wide, narrow, ky, total, places)...  79.4 us
    pallas_call x1, Pallas kernels, on_device(): pl.pallas_call(functools.partial(finish, kk), out_shape=(grid_like, weigh...  5.27 us

profile of v6, /device:TPU:1, one launch (start us, length us, event | category | flops | bytes accessed | tf_op | source)
XLA Modules:
  0.0 85.3 jit_solution(2200415768111402430)
XLA Ops:
  0.6 79.4 %spectral_layer.1 = (bf16[32,8,16,128]{3,2,1,0:T(8,128)(2,1)}, bf16[3,6,48,2048]{3,2,1,0:T(8,128)(2,1)}, bf16[16,3,16,512]{3,2,1,0:T(8,128)(2,1)}, f32[8,512,128]{2,1,0:T(8,128)}) custom-call(bf16[32,8,16,128]{3,2,1,0:T(8,128)(2,1)} %field_hbm.1, bf16[32,8,16,128]{3,2,1,0:T(8,128)(2,1)} %cot_hbm.1, bf16[3,6,48,2048]{3,2,1,0:T(8,128)(2,1)} %weight_hbm.1, ...), custom_call_target="tpu_custom_call" | custom-call | tf_op jit(solution)/shard_map/spectral_layer/pallas_call | solution.py:580
  80.0 5.3 %field_gradient.1 = (bf16[32,8,16,128]{3,2,1,0:T(8,128)(2,1)}, bf16[3,6,48,2048]{3,2,1,0:T(8,128)(2,1)}, bf16[32,8,16,128]{3,2,1,0:T(8,128)(2,1)}) custom-call(bf16[32,8,16,128]{3,2,1,0:T(8,128)(2,1)} %get-tuple-element.10.act_in, bf16[3,6,48,2048]{3,2,1,0:T(8,128)(2,1)} %get-tuple-element.11.wgrad_in, bf16[16,3,16,512]{3,2,1,0:T(8,128)(2,1)} %get-tuple-element.12.back_hbm, ...), custom_call_target="tpu_custom_call" | custom-call | tf_op jit(solution)/shard_map/field_gradient/pallas_call | solution.py:636

commit v7 on v6

--- a/solution.py
+++ b/solution.py
@@ -14,6 +14,7 @@
 YL = 16
 KXL = 6
 KL = 3
+HALVES = 2
 NZ = 128
 VMEM_BYTES = 64 * 1024 * 1024
 MESH = pl.DeviceIdType.MESH
@@ -39,12 +40,13 @@
     cx, sx = angles(nx, kx, True)
     cy, sy = angles(ny, ky, True)
     cz, sz = angles(NZ, kz, False)
-    z_rows = np.stack([cz, -sz], axis=-1).reshape(NZ, wide, KL, 2)
-    z_fwd = z_rows.transpose(2, 1, 3, 0).reshape(KL * wide * 2, NZ)
+    v = wide // HALVES
+    z_rows = np.stack([cz, -sz], axis=-1).reshape(NZ, HALVES, v, KL, 2)
+    z_fwd = z_rows.transpose(3, 2, 1, 4, 0).reshape(KL * wide * 2, NZ)
     fwd = lambda c, s: np.stack([np.stack([c, s]), np.stack([-s, c])])
     inv = lambda c, s: np.stack([np.stack([c, -s]), np.stack([s, c])])
-    fx = fwd(cx, sx).reshape(2, 2, wide, XL, narrow, KXL)
-    x_fwd = fx.transpose(5, 0, 4, 2, 1, 3).reshape(KXL * 2 * narrow, wide * 2 * XL)
+    fx = fwd(cx, sx).reshape(2, 2, HALVES, v, XL, narrow, KXL)
+    x_fwd = fx.transpose(2, 6, 0, 5, 3, 1, 4).reshape(HALVES * KXL * 2 * narrow, v * 2 * XL)
     ix = inv(cx, sx).reshape(2, 2, wide, XL, narrow, KXL)
     x_inv = ix.transpose(2, 0, 3, 5, 1, 4).reshape(wide * 2 * XL, KXL * 2 * narrow)
     fy = fwd(cy, sy).reshape(2, 2, narrow, YL, ky)
@@ -120,25 +122,27 @@
             )
         )
     ]
-    for load in loads:
+    for load in loads[:5]:
         load.start()
 
+    side = wide // HALVES
+    h, v = w // side, lax.rem(w, side)
+    plane = HALVES * narrow
+    here = h * narrow + n
+
     barrier = pltpu.get_barrier_semaphore()
 
-    half = narrow // 2
-    flip = lax.rem(n + half, narrow)
-
-    @pl.loop(0, wide)
-    def _(d):
-        pl.semaphore_signal(
-            barrier, inc=1, device_id={"wide": d, "narrow": flip}, device_id_type=MESH
-        )
-
-    @pl.loop(1, narrow)
-    def _(d):
-        pl.semaphore_signal(
-            barrier, inc=1, device_id={"narrow": lax.rem(n + d, narrow)}, device_id_type=MESH
-        )
+    def along(d):
+        to = lax.rem(v + d, side)
+        return to, {"wide": h * side + to}
+
+    def across(d):
+        to = lax.rem(here + d, plane)
+        return to, {"wide": to // narrow * side + v, "narrow": lax.rem(to, narrow)}
+
+    for count, peer in ((side, along), (plane, across)):
+        for d in range(1, count):
+            pl.semaphore_signal(barrier, inc=1, device_id=peer(d)[1], device_id_type=MESH)
 
     row = lax.broadcasted_iota(jnp.int32, (cells, cells), 0)
     col = lax.broadcasted_iota(jnp.int32, (cells, cells), 1)
@@ -172,16 +176,15 @@
         for i in range(2):
             zs[2 * hb + i, pl.ds(x, kk, stride=XL), :] = out[:, i * 128 : (i + 1) * 128]
 
-    def send_wide(src, dst, send_sem, recv_sem):
-        @pl.loop(0, wide)
-        def _(d):
-            to = lax.rem(w + d, wide)
+    def send(peer, count, src, dst, send_sem, recv_sem):
+        for d in range(1, count):
+            to, device = peer(d)
             pltpu.make_async_remote_copy(
                 src_ref=src(to),
-                dst_ref=dst(w),
+                dst_ref=dst,
                 send_sem=send_sem,
                 recv_sem=recv_sem,
-                device_id={"wide": to, "narrow": flip},
+                device_id=device,
                 device_id_type=MESH,
             ).start()
 
@@ -189,42 +192,36 @@
         pltpu.make_async_copy(ref, ref, sem).wait()
 
     def send_first(a, hb):
-        send_wide(
-            lambda to: fs.at[a, to, hb], lambda me: fr.at[a, me, hb],
+        fr[a, v, hb] = fs[a, v, hb]
+        send(
+            along, side, lambda to: fs.at[a, to, hb], fr.at[a, v, hb],
             fs_sem.at[a, hb], fr_sem.at[a, hb],
         )
 
     def wait_first(buffer, sem, a, hb):
-        wait(buffer.at[a, pl.ds(0, wide), hb], sem.at[a, hb])
+        wait(buffer.at[a, pl.ds(0, side - 1), hb], sem.at[a, hb])
 
     chunks = (pl.ds(0, KL - 1), pl.ds(KL - 1, 1))
 
     def send_last(a, c):
-        send_wide(
-            lambda to: ls.at[a, to, chunks[c]], lambda me: lr.at[a, me, chunks[c]],
+        lr[a, v, chunks[c]] = ls[a, v, chunks[c]]
+        send(
+            along, side, lambda to: ls.at[a, to, chunks[c]], lr.at[a, v, chunks[c]],
             ls_sem.at[a, c], lr_sem.at[a, c],
         )
 
     def wait_last(buffer, sem, a, c):
-        wait(buffer.at[a, pl.ds(0, wide), chunks[c]], sem.at[a, c])
-
-    def send_narrow(a, i, j, take, slot):
-        nr[a, i, j, slot] = ns[a, i, j, take(n)]
-
-        @pl.loop(1, narrow)
-        def _(d):
-            to = lax.rem(n + d, narrow)
-            pltpu.make_async_remote_copy(
-                src_ref=ns.at[a, i, j, take(to)],
-                dst_ref=nr.at[a, i, j, slot],
-                send_sem=ns_sem.at[a, i, j],
-                recv_sem=nr_sem.at[a, i, j],
-                device_id={"narrow": to},
-                device_id_type=MESH,
-            ).start()
+        wait(buffer.at[a, pl.ds(0, side - 1), chunks[c]], sem.at[a, c])
+
+    def send_narrow(a, i, j, take):
+        nr[a, i, j, here] = ns[a, i, j, take(here)]
+        send(
+            across, plane, lambda to: ns.at[a, i, j, take(to)], nr.at[a, i, j, here],
+            ns_sem.at[a, i, j], nr_sem.at[a, i, j],
+        )
 
     def wait_narrow(buffer, sem, a, i, j):
-        wait(buffer.at[a, i, j, pl.ds(0, narrow - 1)], sem.at[a, i, j])
+        wait(buffer.at[a, i, j, pl.ds(0, plane - 1)], sem.at[a, i, j])
 
     def part(j):
         return pl.ds(pl.multiple_of(j * rows_j, rows_j), rows_j)
@@ -233,35 +230,55 @@
         @pl.loop(0, KL)
         def _(j):
             for i in range(2):
-                block = zs[2 * hb + i, part(j), :].astype(BF16).reshape(wide, 2 * XL, 128)
+                block = zs[2 * hb + i, part(j), :].astype(BF16).reshape(side, HALVES * 2 * XL, 128)
                 fs[a, :, hb, j, :, i * 128 : (i + 1) * 128] = block
 
         send_first(a, hb)
 
+    def half_lines(i):
+        return slice(i * 2 * XL, (i + 1) * 2 * XL)
+
+    def own_half(place):
+        first, rows, columns = place
+        rows = rows // HALVES
+        return table[pl.ds(first + h * rows, rows), :columns]
+
     def x_forward(a, j):
-        block = [fr[a, :, hb, j].reshape(rows_j, 256) for hb in range(2)]
-        out = dot(x_fwd(), jnp.concatenate(block, axis=1))
-        out = dot(out.astype(BF16), perm[...])
-        for yb in range(4):
-
-            def piece(kx, ri):
-                first = (kx * 2 + ri) * narrow
-                return out[first : first + narrow, yb * 128 : (yb + 1) * 128]
-
-            for ri in range(2):
-                for g, value in enumerate(transpose_groups([piece(s, ri) for s in range(4)])):
-                    t1[pl.ds(ri * YL + 4 * yb + g, narrow, stride=2 * YL), :] = value
-            last = transpose_groups([piece(4 + s % 2, s // 2) for s in range(4)])
-            for g, value in enumerate(last):
-                t1_last[pl.ds(4 * yb + g, narrow, stride=YL), :] = value
-        ns[a, 0, j, :, : 2 * YL, :] = t1[...].astype(BF16).reshape(narrow, 2 * YL, 128)
-        ns[a, 0, j, :, 2 * YL :, :] = t1_last[...].astype(BF16).reshape(narrow, YL, 128)
-        send_narrow(a, 0, j, lambda to: to, flip)
+        matrix = own_half(places[1])
+        outs = []
+        for to_h in range(HALVES):
+            block = [
+                fr[a, :, hb, j, half_lines(to_h), :].reshape(side * 2 * XL, 256) for hb in range(2)
+            ]
+            outs.append(dot(matrix, jnp.concatenate(block, axis=1)).astype(BF16))
+        both = dot(jnp.concatenate(outs, axis=0), perm[...])
+        rows = KXL * 2 * narrow
+        for to_h in range(HALVES):
+            out = both[to_h * rows : (to_h + 1) * rows]
+            for yb in range(4):
+
+                def piece(kx, ri):
+                    first = (kx * 2 + ri) * narrow
+                    return out[first : first + narrow, yb * 128 : (yb + 1) * 128]
+
+                for ri in range(2):
+                    for g, value in enumerate(transpose_groups([piece(s, ri) for s in range(4)])):
+                        t1[pl.ds(ri * YL + 4 * yb + g, narrow, stride=2 * YL), :] = value
+                last = transpose_groups([piece(4 + s % 2, s // 2) for s in range(4)])
+                for g, value in enumerate(last):
+                    t1_last[pl.ds(4 * yb + g, narrow, stride=YL), :] = value
+            owners = slice(to_h * narrow, (to_h + 1) * narrow)
+            ns[a, 0, j, owners, : 2 * YL, :] = t1[...].astype(BF16).reshape(narrow, 2 * YL, 128)
+            ns[a, 0, j, owners, 2 * YL :, :] = t1_last[...].astype(BF16).reshape(narrow, YL, 128)
+        send_narrow(a, 0, j, lambda to: to)
 
     def y_forward(a, j):
         wait_narrow(nr, nr_sem, a, 0, j)
-        first = dot(y_fwd(), nr[a, 0, j, :, : 2 * YL, :].reshape(narrow * 2 * YL, 128))
-        both = dot(y_fwd_split(), nr[a, 0, j, :, 2 * YL :, :].reshape(narrow * YL, 128))
+        halves = [slice(i * narrow, (i + 1) * narrow) for i in range(HALVES)]
+        first, both = (
+            sum(dot(matrix, nr[a, 0, j, i, lines, :].reshape(-1, 128)) for i in halves)
+            for matrix, lines in ((y_fwd(), slice(0, 2 * YL)), (y_fwd_split(), slice(2 * YL, None)))
+        )
         last = both[: 2 * ky] + shift(both[2 * ky :], 2)
         for kx in range(KXL):
             source = first if kx < 4 else last
@@ -331,33 +348,44 @@
 
     def y_inverse(a, j):
         first = dot(y_inv(), mix[0]).astype(BF16)
-        ns[a, 1, j, :, : 2 * YL, :] = first.reshape(narrow, 2 * YL, 128)
+        ns[a, 1, j, :narrow, : 2 * YL, :] = first.reshape(narrow, 2 * YL, 128)
         both = dot(y_inv_split(), mix[1])
         split = narrow * YL
         last = jnp.where(lane < 2, both[:split], shift(both[split:], 2)).astype(BF16)
-        ns[a, 1, j, :, 2 * YL :, :] = last.reshape(narrow, YL, 128)
-        send_narrow(a, 1, j, lambda to: lax.rem(to + half, narrow), n)
+        ns[a, 1, j, :narrow, 2 * YL :, :] = last.reshape(narrow, YL, 128)
+        send_narrow(a, 1, j, lambda to: lax.rem(to, narrow))
 
     def x_inverse(a, j):
         wait_narrow(nr, nr_sem, a, 1, j)
-        t1[...] = nr[a, 1, j, :, : 2 * YL, :].reshape(narrow * 2 * YL, 128).astype(F32)
-        t1_last[...] = nr[a, 1, j, :, 2 * YL :, :].reshape(narrow * YL, 128).astype(F32)
-        for yb in range(4):
-            lanes = slice(yb * 128, (yb + 1) * 128)
-            ys = [4 * yb + g for g in range(4)]
-            loaded = [
-                [t1[pl.ds(ri * YL + y, narrow, stride=2 * YL), :] for y in ys] for ri in range(2)
-            ]
-            last = [t1_last[pl.ds(y, narrow, stride=YL), :] for y in ys]
-            real, imag, last = [transpose_groups(p) for p in loaded + [last]]
-            pairs = list(zip(real, imag)) + [(last[0], last[2]), (last[1], last[3])]
-            for kx, pair in enumerate(pairs):
-                t2[kx * 2 * narrow : (kx + 1) * 2 * narrow, lanes] = jnp.concatenate(
-                    pair, axis=0
-                ).astype(BF16)
+        rows = KXL * 2 * narrow
+        for from_h in range(HALVES):
+            owners = slice(from_h * narrow, (from_h + 1) * narrow)
+            t1[...] = nr[a, 1, j, owners, : 2 * YL, :].reshape(narrow * 2 * YL, 128).astype(F32)
+            t1_last[...] = nr[a, 1, j, owners, 2 * YL :, :].reshape(narrow * YL, 128).astype(F32)
+            for yb in range(4):
+                lanes = slice(yb * 128, (yb + 1) * 128)
+                ys = [4 * yb + g for g in range(4)]
+                loaded = [
+                    [t1[pl.ds(ri * YL + y, narrow, stride=2 * YL), :] for y in ys] for ri in range(2)
+                ]
+                last = [t1_last[pl.ds(y, narrow, stride=YL), :] for y in ys]
+                real, imag, last = [transpose_groups(p) for p in loaded + [last]]
+                pairs = list(zip(real, imag)) + [(last[0], last[2]), (last[1], last[3])]
+                for kx, pair in enumerate(pairs):
+                    first = from_h * rows + kx * 2 * narrow
+                    t2[first : first + 2 * narrow, lanes] = jnp.concatenate(pair, axis=0).astype(BF16)
         modes_cy = dot(t2[...], perm_t[...]).astype(BF16)
-        out = dot(x_inv(), modes_cy).astype(BF16)
-        ls[a, :, j] = out.reshape(wide, 2 * XL, cells)
+        matrix = own_half(places[2])
+        for from_h in range(HALVES):
+            out = dot(matrix, modes_cy[from_h * rows : (from_h + 1) * rows]).astype(BF16)
+            ls[a, :, j, half_lines(from_h), :] = out.reshape(side, 2 * XL, cells)
+
+    def store_gradient(j):
+        return pltpu.make_async_copy(wgrad.at[j], wgrad_hbm.at[j], store_sem.at[4 + j])
+
+    def make_gradient(j):
+        weight_gradient(j)
+        store_gradient(j).start()
 
     def each(step):
         @pl.loop(0, KL)
@@ -381,7 +409,7 @@
 
                 @pl.when(j == KL - 1)
                 def _():
-                    weight_gradient(0)
+                    make_gradient(0)
 
             x_inverse(a, j)
 
@@ -392,7 +420,7 @@
                     send_last(a, c)
 
         if a:
-            pl.loop(1, KL)(weight_gradient)
+            pl.loop(1, KL)(make_gradient)
 
     def depth_in():
         for c in range(2):
@@ -418,9 +446,11 @@
         for x in range(XL):
             depth(x, hb, field[hb * 16 : (hb + 1) * 16, x].reshape(256, NZ))
         if hb == 0:
-            pl.semaphore_wait(barrier, wide + narrow - 1)
+            pl.semaphore_wait(barrier, side + plane - 2)
         depth_out(0, hb)
 
+    for load in loads[5:]:
+        load.start()
     loads[3].wait()
     loads[4].wait()
     perm[...] = ones_where(((row & 15) == (col >> 5)) & ((row >> 4) == (col & 31)))
@@ -482,7 +512,6 @@
             (
                 (act, act_hbm),
                 (near, near_hbm),
-                (wgrad, wgrad_hbm),
                 (lr.at[1, :, chunks[0]], back_hbm.at[:, chunks[0]]),
                 (lr.at[1, :, chunks[1]], back_hbm.at[:, chunks[1]]),
             )
@@ -492,10 +521,9 @@
     pointwise(pw_back, slope)
     stores[1].start()
     through_modes(1)
-    stores[2].start()
     for c in range(2):
         wait_last(lr, lr_sem, 1, c)
-        stores[3 + c].start()
+        stores[2 + c].start()
 
     for a in range(2):
         for i in range(2):
@@ -504,6 +532,7 @@
             for j in range(KL):
                 wait_narrow(ns, ns_sem, a, i, j)
 
+    each(lambda j: store_gradient(j).wait())
     for store in stores:
         store.wait()
 
@@ -545,7 +574,7 @@
             load.wait()
         for b in (2 * hb, 2 * hb + 1):
             for j in range(KL):
-                rows = back.shape[0] * 2 * XL
+                rows = back.shape[0] * back.shape[2]
                 block = back[:, j, :, b * 128 : (b + 1) * 128].reshape(rows, 128)
                 zi[b, j * rows : (j + 1) * rows, :] = block.astype(F32)
         for x in range(XL):
@@ -574,6 +603,7 @@
     cells = C * YL
     kk = KL * wide * 2
     modes = KXL * 2 * ky
+    side, plane = wide // HALVES, narrow * HALVES
     hbm = pl.BlockSpec(memory_space=pl.ANY)
     grid_like = jax.ShapeDtypeStruct(field.shape, BF16)
     weight_like = jax.ShapeDtypeStruct(weight.shape, BF16)
@@ -582,7 +612,7 @@
         out_shape=(
             grid_like,
             weight_like,
-            jax.ShapeDtypeStruct((wide, KL, 2 * XL, cells), BF16),
+            jax.ShapeDtypeStruct((side, KL, HALVES * 2 * XL, cells), BF16),
             jax.ShapeDtypeStruct((XL, cells, NZ), F32),
         ),
         in_specs=[hbm] * 5,
@@ -605,7 +635,7 @@
             pltpu.VMEM((2, 2 * ky, 128), BF16),
             pltpu.VMEM((narrow * 2 * YL, 128), F32),
             pltpu.VMEM((narrow * YL, 128), F32),
-            pltpu.VMEM((KXL * narrow * 2, cells), BF16),
+            pltpu.VMEM((HALVES * KXL * narrow * 2, cells), BF16),
             pltpu.VMEM((cells, cells), BF16),
             pltpu.VMEM((cells, cells), BF16),
             pltpu.VMEM((cells, cells), BF16),
@@ -613,12 +643,12 @@
             pltpu.VMEM((128, 1024), BF16),
             pltpu.VMEM((128, 128), BF16),
             pltpu.VMEM((1024, 128), BF16),
-            pltpu.VMEM((2, wide, 2, KL, 2 * XL, 256), BF16),
-            pltpu.VMEM((2, wide, 2, KL, 2 * XL, 256), BF16),
-            pltpu.VMEM((2, wide, KL, 2 * XL, cells), BF16),
-            pltpu.VMEM((2, wide, KL, 2 * XL, cells), BF16),
-            pltpu.VMEM((2, 2, KL, narrow, 3 * YL, 128), BF16),
-            pltpu.VMEM((2, 2, KL, narrow, 3 * YL, 128), BF16),
+            pltpu.VMEM((2, side, 2, KL, HALVES * 2 * XL, 256), BF16),
+            pltpu.VMEM((2, side, 2, KL, HALVES * 2 * XL, 256), BF16),
+            pltpu.VMEM((2, side, KL, HALVES * 2 * XL, cells), BF16),
+            pltpu.VMEM((2, side, KL, HALVES * 2 * XL, cells), BF16),
+            pltpu.VMEM((2, 2, KL, plane, 3 * YL, 128), BF16),
+            pltpu.VMEM((2, 2, KL, plane, 3 * YL, 128), BF16),
             pltpu.SemaphoreType.DMA((2, 2)),
             pltpu.SemaphoreType.DMA((2, 2)),
             pltpu.SemaphoreType.DMA((2, 2)),
@@ -626,7 +656,7 @@
             pltpu.SemaphoreType.DMA((2, 2, KL)),
             pltpu.SemaphoreType.DMA((2, 2, KL)),
             pltpu.SemaphoreType.DMA((7,)),
-            pltpu.SemaphoreType.DMA((5,)),
+            pltpu.SemaphoreType.DMA((4 + KL,)),
         ],
         compiler_params=pltpu.CompilerParams(
             collective_id=0, has_side_effects=True, vmem_limit_bytes=VMEM_BYTES
@@ -639,7 +669,7 @@
         in_specs=[hbm] * 5,
         out_specs=(hbm,) * 3,
         scratch_shapes=[
-            pltpu.VMEM((wide, KL, 2 * XL, cells), BF16),
+            pltpu.VMEM((side, KL, HALVES * 2 * XL, cells), BF16),
             pltpu.VMEM((XL, cells, NZ), F32),
             pltpu.VMEM((kk, NZ), BF16),
             pltpu.VMEM((4, kk * XL, 128), F32),

time: 85.4 us -> 89.4 us (1.047)
  Pallas kernels: 84.6 us -> 88.6 us
    pallas_call x1, Pallas kernels: 79.4 us -> 83.4 us  [on_device(): pl.pallas_call(functools.partial(kernel, wide, narrow, ky, total, places)...]
where the time goes in v7:
time: 89.4 us; the launch traced here: 89.3 us
  Pallas kernels  88.6 us (99%)
    pallas_call x1, Pallas kernels, on_device(): pl.pallas_call(functools.partial(kernel, wide, narrow, ky, total, places)...  83.4 us
    pallas_call x1, Pallas kernels, on_device(): pl.pallas_call(functools.partial(finish, kk), out_shape=(grid_like, weigh...  5.27 us

profile of v7, /device:TPU:1, one launch (start us, length us, event | category | flops | bytes accessed | tf_op | source)
XLA Modules:
  0.0 89.3 jit_solution(16828092960224718699)
XLA Ops:
  0.6 83.4 %spectral_layer.1 = (bf16[32,8,16,128]{3,2,1,0:T(8,128)(2,1)}, bf16[3,6,48,2048]{3,2,1,0:T(8,128)(2,1)}, bf16[8,3,32,512]{3,2,1,0:T(8,128)(2,1)}, f32[8,512,128]{2,1,0:T(8,128)}) custom-call(bf16[32,8,16,128]{3,2,1,0:T(8,128)(2,1)} %field_hbm.1, bf16[32,8,16,128]{3,2,1,0:T(8,128)(2,1)} %cot_hbm.1, bf16[3,6,48,2048]{3,2,1,0:T(8,128)(2,1)} %weight_hbm.1, ...), custom_call_target="tpu_custom_call" | custom-call | tf_op jit(solution)/shard_map/spectral_layer/pallas_call | solution.py:610
  84.0 5.3 %field_gradient.1 = (bf16[32,8,16,128]{3,2,1,0:T(8,128)(2,1)}, bf16[3,6,48,2048]{3,2,1,0:T(8,128)(2,1)}, bf16[32,8,16,128]{3,2,1,0:T(8,128)(2,1)}) custom-call(bf16[32,8,16,128]{3,2,1,0:T(8,128)(2,1)} %get-tuple-element.10.act_in, bf16[3,6,48,2048]{3,2,1,0:T(8,128)(2,1)} %get-tuple-element.11.wgrad_in, bf16[8,3,32,512]{3,2,1,0:T(8,128)(2,1)} %get-tuple-element.12.back_hbm, ...), custom_call_target="tpu_custom_call" | custom-call | tf_op jit(solution)/shard_map/field_gradient/pallas_call | solution.py:666

commit v8 on v6

--- a/solution.py
+++ b/solution.py
@@ -120,7 +120,7 @@
             )
         )
     ]
-    for load in loads:
+    for load in loads[:5]:
         load.start()
 
     barrier = pltpu.get_barrier_semaphore()
@@ -359,6 +359,13 @@
         out = dot(x_inv(), modes_cy).astype(BF16)
         ls[a, :, j] = out.reshape(wide, 2 * XL, cells)
 
+    def store_gradient(j):
+        return pltpu.make_async_copy(wgrad.at[j], wgrad_hbm.at[j], store_sem.at[4 + j])
+
+    def make_gradient(j):
+        weight_gradient(j)
+        store_gradient(j).start()
+
     def each(step):
         @pl.loop(0, KL)
         def _(j):
@@ -381,7 +388,7 @@
 
                 @pl.when(j == KL - 1)
                 def _():
-                    weight_gradient(0)
+                    make_gradient(0)
 
             x_inverse(a, j)
 
@@ -392,7 +399,7 @@
                     send_last(a, c)
 
         if a:
-            pl.loop(1, KL)(weight_gradient)
+            pl.loop(1, KL)(make_gradient)
 
     def depth_in():
         for c in range(2):
@@ -421,6 +428,8 @@
             pl.semaphore_wait(barrier, wide + narrow - 1)
         depth_out(0, hb)
 
+    for load in loads[5:]:
+        load.start()
     loads[3].wait()
     loads[4].wait()
     perm[...] = ones_where(((row & 15) == (col >> 5)) & ((row >> 4) == (col & 31)))
@@ -482,7 +491,6 @@
             (
                 (act, act_hbm),
                 (near, near_hbm),
-                (wgrad, wgrad_hbm),
                 (lr.at[1, :, chunks[0]], back_hbm.at[:, chunks[0]]),
                 (lr.at[1, :, chunks[1]], back_hbm.at[:, chunks[1]]),
             )
@@ -492,10 +500,9 @@
     pointwise(pw_back, slope)
     stores[1].start()
     through_modes(1)
-    stores[2].start()
     for c in range(2):
         wait_last(lr, lr_sem, 1, c)
-        stores[3 + c].start()
+        stores[2 + c].start()
 
     for a in range(2):
         for i in range(2):
@@ -504,6 +511,7 @@
             for j in range(KL):
                 wait_narrow(ns, ns_sem, a, i, j)
 
+    each(lambda j: store_gradient(j).wait())
     for store in stores:
         store.wait()
 
@@ -626,7 +634,7 @@
             pltpu.SemaphoreType.DMA((2, 2, KL)),
             pltpu.SemaphoreType.DMA((2, 2, KL)),
             pltpu.SemaphoreType.DMA((7,)),
-            pltpu.SemaphoreType.DMA((5,)),
+            pltpu.SemaphoreType.DMA((4 + KL,)),
         ],
         compiler_params=pltpu.CompilerParams(
             collective_id=0, has_side_effects=True, vmem_limit_bytes=VMEM_BYTES

time: 85.4 us -> 85.8 us (level)
  no operation moved by 1% of the time
where the time goes in v8:
time: 85.8 us; the launch traced here: 85.7 us
  Pallas kernels  85 us (99%)
    pallas_call x1, Pallas kernels, on_device(): pl.pallas_call(functools.partial(kernel, wide, narrow, ky, total, places)...  79.8 us
    pallas_call x1, Pallas kernels, on_device(): pl.pallas_call(functools.partial(finish, kk), out_shape=(grid_like, weigh...  5.27 us

profile of v8, /device:TPU:1, one launch (start us, length us, event | category | flops | bytes accessed | tf_op | source)
XLA Modules:
  0.0 85.7 jit_solution(13736530097862392939)
XLA Ops:
  0.6 79.8 %spectral_layer.1 = (bf16[32,8,16,128]{3,2,1,0:T(8,128)(2,1)}, bf16[3,6,48,2048]{3,2,1,0:T(8,128)(2,1)}, bf16[16,3,16,512]{3,2,1,0:T(8,128)(2,1)}, f32[8,512,128]{2,1,0:T(8,128)}) custom-call(bf16[32,8,16,128]{3,2,1,0:T(8,128)(2,1)} %field_hbm.1, bf16[32,8,16,128]{3,2,1,0:T(8,128)(2,1)} %cot_hbm.1, bf16[3,6,48,2048]{3,2,1,0:T(8,128)(2,1)} %weight_hbm.1, ...), custom_call_target="tpu_custom_call" | custom-call | tf_op jit(solution)/shard_map/spectral_layer/pallas_call | solution.py:588
  80.4 5.3 %field_gradient.1 = (bf16[32,8,16,128]{3,2,1,0:T(8,128)(2,1)}, bf16[3,6,48,2048]{3,2,1,0:T(8,128)(2,1)}, bf16[32,8,16,128]{3,2,1,0:T(8,128)(2,1)}) custom-call(bf16[32,8,16,128]{3,2,1,0:T(8,128)(2,1)} %get-tuple-element.10.act_in, bf16[3,6,48,2048]{3,2,1,0:T(8,128)(2,1)} %get-tuple-element.11.wgrad_in, bf16[16,3,16,512]{3,2,1,0:T(8,128)(2,1)} %get-tuple-element.12.back_hbm, ...), custom_call_target="tpu_custom_call" | custom-call | tf_op jit(solution)/shard_map/field_gradient/pallas_call | solution.py:644

commit v9 on v8

--- a/solution.py
+++ b/solution.py
@@ -422,8 +422,10 @@
     loads[1].wait()
     for hb in range(2):
         loads[2 * hb].wait()
-        for x in range(XL):
+        @pl.loop(0, XL, unroll=2)
+        def _(x):
             depth(x, hb, field[hb * 16 : (hb + 1) * 16, x].reshape(256, NZ))
+
         if hb == 0:
             pl.semaphore_wait(barrier, wide + narrow - 1)
         depth_out(0, hb)
@@ -464,7 +466,9 @@
     def _(hb):
         rows = pl.ds(pl.multiple_of(hb * 256, 256), 256)
         group = pl.ds(hb * 16, 16)
-        for x in range(XL):
+
+        @pl.loop(0, XL, unroll=2)
+        def _(x):
             block = jnp.concatenate(
                 [zi[2 * hb + i, pl.ds(x, kk, stride=XL), :].astype(BF16) for i in range(2)], axis=1
             )

time: 85.8 us -> 86.6 us (level)
  Pallas kernels: 85 us -> 85.9 us
where the time goes in v9:
time: 86.6 us; the launch traced here: 86.5 us
  Pallas kernels  85.9 us (99%)
    pallas_call x1, Pallas kernels, on_device(): pl.pallas_call(functools.partial(kernel, wide, narrow, ky, total, places)...  80.6 us
    pallas_call x1, Pallas kernels, on_device(): pl.pallas_call(functools.partial(finish, kk), out_shape=(grid_like, weigh...  5.27 us

profile of v9, /device:TPU:1, one launch (start us, length us, event | category | flops | bytes accessed | tf_op | source)
XLA Modules:
  0.0 86.5 jit_solution(11158588451201888224)
XLA Ops:
  0.6 80.6 %spectral_layer.1 = (bf16[32,8,16,128]{3,2,1,0:T(8,128)(2,1)}, bf16[3,6,48,2048]{3,2,1,0:T(8,128)(2,1)}, bf16[16,3,16,512]{3,2,1,0:T(8,128)(2,1)}, f32[8,512,128]{2,1,0:T(8,128)}) custom-call(bf16[32,8,16,128]{3,2,1,0:T(8,128)(2,1)} %field_hbm.1, bf16[32,8,16,128]{3,2,1,0:T(8,128)(2,1)} %cot_hbm.1, bf16[3,6,48,2048]{3,2,1,0:T(8,128)(2,1)} %weight_hbm.1, ...), custom_call_target="tpu_custom_call" | custom-call | tf_op jit(solution)/shard_map/spectral_layer/pallas_call | solution.py:592
  81.2 5.3 %field_gradient.1 = (bf16[32,8,16,128]{3,2,1,0:T(8,128)(2,1)}, bf16[3,6,48,2048]{3,2,1,0:T(8,128)(2,1)}, bf16[32,8,16,128]{3,2,1,0:T(8,128)(2,1)}) custom-call(bf16[32,8,16,128]{3,2,1,0:T(8,128)(2,1)} %get-tuple-element.10.act_in, bf16[3,6,48,2048]{3,2,1,0:T(8,128)(2,1)} %get-tuple-element.11.wgrad_in, bf16[16,3,16,512]{3,2,1,0:T(8,128)(2,1)} %get-tuple-element.12.back_hbm, ...), custom_call_target="tpu_custom_call" | custom-call | tf_op jit(solution)/shard_map/field_gradient/pallas_call | solution.py:648
